TPU v7x, 32 devices: a whole 2x2x4 slice. The times are simulated.
32 devices in a mesh: dp: 8 (over z, y), tensor: 4 (over x, core).
Axes of the slice: x: 2, y: 2, z: 4, core: 2. Of those that a mesh axis runs over, the one named last changes fastest.
Arguments:
- stream: float32 [8192, 1024], P(('dp', 'tensor')), may hold values from -6 to 6
- cotangent: float32 [8192, 1024], P(('dp', 'tensor')), may hold values from -15 to 15
- lengths: int32 [8, 3], P('dp'), may hold values from 1 to 896, 1024 in all within a row
- routes: int32 [8192, 8], P('dp'), may hold values from 0 to 31, all different within a row; in each aligned block of 1024 rows (0 to 1023, 1024 to 2047, ...) at most 512 rows name the same one
- query_weight: float32 [1024, 1024], P('dp', 'tensor'), may hold values from -0.1875 to 0.1875
- query_moment: float32 [1024, 1024], P('dp', 'tensor'), may hold values from -96 to 96
- query_second: float32 [1024, 1024], P('dp', 'tensor'), may hold values from 983.04 to 3932.16
- key_value_weight: float32 [2, 1024, 512], P(None, 'dp', 'tensor'), may hold values from -0.1875 to 0.1875
- key_value_moment: float32 [2, 1024, 512], P(None, 'dp', 'tensor'), may hold values from -96 to 96
- key_value_second: float32 [2, 1024, 512], P(None, 'dp', 'tensor'), may hold values from 983.04 to 3932.16
- output_weight: float32 [1024, 1024], P('tensor', 'dp'), may hold values from -4 to 4
- output_moment: float32 [1024, 1024], P('tensor', 'dp'), may hold values from -6 to 6
- output_second: float32 [1024, 1024], P('tensor', 'dp'), may hold values from 3.6 to 14.4
- router_weight: float32 [1024, 32], replicated, may hold values from -0.09375 to 0.09375
- router_moment: float32 [1024, 32], replicated, may hold values from -512 to 512
- router_second: float32 [1024, 32], replicated, may hold values from 31129.6 to 124518.4
- gate_up_weight: float32 [2, 32, 1024, 512], P(None, None, 'dp', 'tensor'), may hold values from -0.1875 to 0.1875
- gate_up_moment: float32 [2, 32, 1024, 512], P(None, None, 'dp', 'tensor'), may hold values from -20 to 20
- gate_up_second: float32 [2, 32, 1024, 512], P(None, None, 'dp', 'tensor'), may hold values from 41.6 to 166.4
- down_weight: float32 [32, 512, 1024], P(None, 'tensor', 'dp'), may hold values from -1 to 1
- down_moment: float32 [32, 512, 1024], P(None, 'tensor', 'dp'), may hold values from -4 to 4
- down_second: float32 [32, 512, 1024], P(None, 'tensor', 'dp'), may hold values from 1.76 to 7.04
- norm_gains: float32 [2, 1024], replicated, may hold values from 0.5 to 1.5
- gains_moment: float32 [2, 1024], replicated, may hold values from -128 to 128
- gains_second: float32 [2, 1024], replicated, may hold values from 2048 to 8192
Outputs:
- result: float32 [8192, 1024], P(('dp', 'tensor'))
- stream_grad: float32 [8192, 1024], P(('dp', 'tensor'))
- new_query_moment: float32 [1024, 1024], P('dp', 'tensor')
- new_query_second: float32 [1024, 1024], P('dp', 'tensor')
- new_query_weight: float32 [1024, 1024], P('dp', 'tensor')
- new_key_value_moment: float32 [2, 1024, 512], P(None, 'dp', 'tensor')
- new_key_value_second: float32 [2, 1024, 512], P(None, 'dp', 'tensor')
- new_key_value_weight: float32 [2, 1024, 512], P(None, 'dp', 'tensor')
- new_output_moment: float32 [1024, 1024], P('tensor', 'dp')
- new_output_second: float32 [1024, 1024], P('tensor', 'dp')
- new_output_weight: float32 [1024, 1024], P('tensor', 'dp')
- new_router_moment: float32 [1024, 32], replicated
- new_router_second: float32 [1024, 32], replicated
- new_router_weight: float32 [1024, 32], replicated
- new_gate_up_moment: float32 [2, 32, 1024, 512], P(None, None, 'dp', 'tensor')
- new_gate_up_second: float32 [2, 32, 1024, 512], P(None, None, 'dp', 'tensor')
- new_gate_up_weight: float32 [2, 32, 1024, 512], P(None, None, 'dp', 'tensor')
- new_down_moment: float32 [32, 512, 1024], P(None, 'tensor', 'dp')
- new_down_second: float32 [32, 512, 1024], P(None, 'tensor', 'dp')
- new_down_weight: float32 [32, 512, 1024], P(None, 'tensor', 'dp')
- new_gains_moment: float32 [2, 1024], replicated
- new_gains_second: float32 [2, 1024], replicated
- new_norm_gains: float32 [2, 1024], replicated
Inputs may be any that keep to these rules, and one draw needn't show every extreme that they name: `lengths`: the longest sequence of each group has exactly 896 tokens. `routes`: each token names 8 different experts; within each aligned block of 1024 rows (one group) no expert is named by more than 512 rows, and in some block some expert is named by exactly 512.
All inputs are finite; a program needn't handle non-finite values.
Results may differ from a plain program's by a relative error of at most 0.015.
The roundings to bfloat16 on the way count: a program that leaves them out, or rounds other values in their place, can miss the bound.
Values may be sent and summed in bfloat16 or wider, within the bound.
No kernel may reach another device: no remote copies, remote signals or barrier semaphores. Data moves between devices by JAX's collectives and lax.ppermute only.
A program may use at most 320 MiB of HBM per device.

v0:
```python
import jax
import jax.numpy as jnp
from jax import lax
from jax.sharding import PartitionSpec as P

D = 1024
H = 16
HD = 64
FF = 512
STEP = 10


EPS = 1e-05
HIGH = lax.Precision.HIGHEST
BETA_ONE = 0.9
BETA_TWO = 0.95
WEIGHT_DECAY = 0.1


def positions(length_row, row_count):
    end_points = jnp.cumsum(length_row)
    start_points = end_points - length_row
    row_index = jnp.arange(row_count, dtype=jnp.int32)
    segment = jnp.sum((row_index[:, None] >= end_points[None, :]).astype(jnp.int32), 1)
    member = segment[:, None] == jnp.arange(length_row.shape[0], dtype=jnp.int32)[None, :]
    position = row_index - jnp.sum(jnp.where(member, start_points[None, :], 0), 1)
    return (segment, position)


def rope_tables(position, half_size):
    frequency = 10000.0 ** (-jnp.arange(half_size, dtype=jnp.float32) / half_size)
    angles = position.astype(jnp.float32)[:, None] * frequency[None, :]
    return (jnp.cos(angles), jnp.sin(angles))


def rotate(vectors, cosine, sine_part):
    half_size = vectors.shape[-1] // 2
    first_half = vectors[..., :half_size]
    second_half = vectors[..., half_size:]
    cosine_rows = cosine[:, None, :]
    sine_rows = sine_part[:, None, :]
    return jnp.concatenate(
        [
            first_half * cosine_rows - second_half * sine_rows,
            second_half * cosine_rows + first_half * sine_rows,
        ],
        -1,
    )


def softmax_rows(scores):
    maximum = jnp.max(scores, -1, keepdims=True)
    exp_scores = jnp.exp(scores - maximum)
    return exp_scores / jnp.sum(exp_scores, -1, keepdims=True)


def route_slots(routes_group, row_count, experts, capacity):
    flat_experts = routes_group.reshape(-1)
    flat_hot = (flat_experts[:, None] == jnp.arange(experts, dtype=jnp.int32)[None, :]).astype(
        jnp.int32
    )
    earlier = jnp.cumsum(flat_hot, 0) - flat_hot
    slot_rank = jnp.sum(earlier * flat_hot, 1)
    flat_index = flat_experts * capacity + slot_rank
    top_count = routes_group.shape[1]
    token_index = jnp.arange(row_count * top_count, dtype=jnp.int32) // top_count
    slot_table = (
        jnp.full((experts * capacity,), row_count, jnp.int32).at[flat_index].set(token_index)
    )
    return (slot_table, flat_index)


def adam_update(weight, gradient, moment, second, step_rate, decay_rate):
    new_moment = BETA_ONE * moment + (1.0 - BETA_ONE) * gradient
    new_second = BETA_TWO * second + (1.0 - BETA_TWO) * gradient * gradient
    moment_hat = new_moment / (1.0 - BETA_ONE**STEP)
    second_hat = new_second / (1.0 - BETA_TWO**STEP)
    new_weight = weight - step_rate * (
        moment_hat / (jnp.sqrt(second_hat) + 1e-08) + decay_rate * weight
    )
    return (new_moment, new_second, new_weight)


def body(
    stream,
    cotangent,
    lengths,
    routes,
    query_weight,
    query_moment,
    query_second,
    key_value_weight,
    key_value_moment,
    key_value_second,
    output_weight,
    output_moment,
    output_second,
    router_weight,
    router_moment,
    router_second,
    gate_up_weight,
    gate_up_moment,
    gate_up_second,
    down_weight,
    down_moment,
    down_second,
    norm_gains,
    gains_moment,
    gains_second,
):
    tensor_size = lax.axis_size("tensor")
    local_rows = stream.shape[0]
    group_rows = local_rows * tensor_size
    offset = lax.axis_index("tensor") * local_rows
    experts = down_weight.shape[0]
    top_count = routes.shape[1]
    capacity = 2 * group_rows * top_count // experts
    block_rows = min(512, group_rows)
    block_total = group_rows // block_rows
    query_heads = query_weight.shape[1] // HD
    pair_heads = key_value_weight.shape[2] // HD
    share_count = query_heads // pair_heads
    score_scale = HD ** (-0.5)
    together = 4
    block_count = experts // together
    segment, position = positions(lengths[0], group_rows)
    cosine, sine_part = rope_tables(position, HD // 2)
    row_index = jnp.arange(group_rows, dtype=jnp.int32)
    query_full, pair_full, output_full = (
        lax.all_gather(query_weight.astype(jnp.bfloat16), "dp", axis=0, tiled=True),
        lax.all_gather(key_value_weight.astype(jnp.bfloat16), "dp", axis=1, tiled=True),
        lax.all_gather(output_weight.astype(jnp.bfloat16), "dp", axis=1, tiled=True),
    )
    scale_one = lax.rsqrt(jnp.mean(stream * stream, -1, keepdims=True) + EPS)
    normed_one = (stream * scale_one * norm_gains[0]).astype(jnp.bfloat16)
    rows_one = lax.all_gather(normed_one, "tensor", axis=0, tiled=True)
    query_raw = jnp.dot(rows_one, query_full, preferred_element_type=jnp.float32).reshape(
        group_rows, query_heads, HD
    )
    pair_raw = jnp.einsum("td,cdf->ctf", rows_one, pair_full, preferred_element_type=jnp.float32)
    queries = (
        rotate(query_raw, cosine, sine_part)
        .astype(jnp.bfloat16)
        .reshape(group_rows, pair_heads, share_count, HD)
    )
    key_rows = rotate(pair_raw[0].reshape(group_rows, pair_heads, HD), cosine, sine_part).astype(
        jnp.bfloat16
    )
    value_rows = pair_raw[1].reshape(group_rows, pair_heads, HD).astype(jnp.bfloat16)

    def block_scores(row_start):
        query_block = queries[row_start : row_start + block_rows]
        segment_block = segment[row_start : row_start + block_rows]
        index_block = row_index[row_start : row_start + block_rows]
        scores = score_scale * jnp.einsum(
            "qkgd,tkd->kgqt", query_block, key_rows, preferred_element_type=jnp.float32
        )
        allowed = (segment_block[:, None] == segment[None, :]) & (
            row_index[None, :] <= index_block[:, None]
        )
        return (jnp.where(allowed, scores, -1e30), query_block)

    log_totals = []
    attended_blocks = []
    for block_index in range(block_total):
        scores, query_block = block_scores(block_index * block_rows)
        maximum = jnp.max(scores, -1, keepdims=True)
        log_total = maximum + jnp.log(jnp.sum(jnp.exp(scores - maximum), -1, keepdims=True))
        probabilities = jnp.exp(scores - log_total)
        attended_blocks.append(
            jnp.einsum(
                "kgqt,tkd->qkgd",
                probabilities.astype(jnp.bfloat16),
                value_rows,
                preferred_element_type=jnp.float32,
            )
        )
        log_totals.append(log_total)
    attended = (
        jnp.concatenate(attended_blocks, 0)
        .reshape(group_rows, query_heads * HD)
        .astype(jnp.bfloat16)
    )
    attention_own = lax.psum_scatter(
        jnp.dot(attended, output_full, preferred_element_type=jnp.float32),
        "tensor",
        scatter_dimension=0,
        tiled=True,
    )
    hidden = stream + attention_own
    scale_two = lax.rsqrt(jnp.mean(hidden * hidden, -1, keepdims=True) + EPS)
    normed_two = (hidden * scale_two * norm_gains[1]).astype(jnp.bfloat16)
    rows_two, back_rows = (
        lax.all_gather(normed_two, "tensor", axis=0, tiled=True),
        lax.all_gather(cotangent.astype(jnp.bfloat16), "tensor", axis=0, tiled=True),
    )
    router_low = router_weight.astype(jnp.bfloat16)
    logits = jnp.dot(rows_two, router_low, preferred_element_type=jnp.float32)
    chosen = (routes[:, :, None] == jnp.arange(experts, dtype=jnp.int32)[None, None, :]).astype(
        jnp.float32
    )
    gate_weights = softmax_rows(jnp.sum(chosen * logits[:, None, :], -1))
    slot_table, flat_index = route_slots(routes, group_rows, experts, capacity)
    slot_gate = (
        jnp.zeros((experts * capacity,), jnp.float32).at[flat_index].set(gate_weights.reshape(-1))
    )
    zero_row = jnp.zeros((1, D), jnp.bfloat16)
    padded_rows = jnp.concatenate([rows_two, zero_row], 0)
    padded_back = jnp.concatenate([back_rows, zero_row], 0)
    zero_sums = jnp.zeros((group_rows + 1, D), jnp.float32)

    def expert_work(running, block_index, gate_up_block, down_block):
        mixed_sum, row_grads = running
        slot_start = block_index * together * capacity
        slots_here = lax.dynamic_slice_in_dim(slot_table, slot_start, together * capacity)
        gates_here = lax.dynamic_slice_in_dim(slot_gate, slot_start, together * capacity).reshape(
            together, capacity, 1
        )
        inputs_here = padded_rows[slots_here].reshape(together, capacity, D)
        back_here = padded_back[slots_here].reshape(together, capacity, D)
        gate_pre = jnp.einsum(
            "ecd,edf->ecf", inputs_here, gate_up_block[0], preferred_element_type=jnp.float32
        )
        up_pre = jnp.einsum(
            "ecd,edf->ecf", inputs_here, gate_up_block[1], preferred_element_type=jnp.float32
        )
        sigmoid_gate = jax.nn.sigmoid(gate_pre)
        active = gate_pre * sigmoid_gate
        middle = (active * up_pre).astype(jnp.bfloat16)
        expert_out = jnp.einsum(
            "ecf,efd->ecd", middle, down_block, preferred_element_type=jnp.float32
        )
        mixed_sum = mixed_sum.at[slots_here].add(
            (gates_here * expert_out).reshape(together * capacity, D)
        )
        slot_gate_grad = jnp.sum(back_here.astype(jnp.float32) * expert_out, -1)
        out_back = (gates_here * back_here).astype(jnp.bfloat16)
        down_grad = jnp.einsum("ecf,ecd->efd", middle, out_back, preferred_element_type=jnp.float32)
        middle_back = jnp.einsum(
            "ecd,efd->ecf", out_back, down_block, preferred_element_type=jnp.float32
        )
        gate_back = (
            middle_back * up_pre * sigmoid_gate * (1.0 + gate_pre * (1.0 - sigmoid_gate))
        ).astype(jnp.bfloat16)
        up_back = (middle_back * active).astype(jnp.bfloat16)
        gate_grad = jnp.einsum(
            "ecd,ecf->edf", inputs_here, gate_back, preferred_element_type=jnp.float32
        )
        up_grad = jnp.einsum(
            "ecd,ecf->edf", inputs_here, up_back, preferred_element_type=jnp.float32
        )
        slot_back = jnp.einsum(
            "ecf,edf->ecd", gate_back, gate_up_block[0], preferred_element_type=jnp.float32
        ) + jnp.einsum(
            "ecf,edf->ecd", up_back, gate_up_block[1], preferred_element_type=jnp.float32
        )
        row_grads = row_grads.at[slots_here].add(slot_back.reshape(together * capacity, D))
        return ((mixed_sum, row_grads), (gate_grad, up_grad, down_grad, slot_gate_grad))

    gate_up_full, down_full = (
        lax.all_gather(gate_up_weight.astype(jnp.bfloat16), "dp", axis=2, tiled=True),
        lax.all_gather(down_weight.astype(jnp.bfloat16), "dp", axis=2, tiled=True),
    )

    def scan_step(running, block_index):
        gate_up_block = lax.dynamic_slice_in_dim(gate_up_full, block_index * together, together, 1)
        down_block = lax.dynamic_slice_in_dim(down_full, block_index * together, together, 0)
        return expert_work(running, block_index, gate_up_block, down_block)

    (mixed_sum, row_grads), (gate_parts, up_parts, down_parts, gate_slots) = lax.scan(
        scan_step, (zero_sums, zero_sums), jnp.arange(block_count, dtype=jnp.int32)
    )
    gate_whole = gate_parts.reshape(experts, gate_parts.shape[2], gate_parts.shape[3])
    up_whole = up_parts.reshape(experts, up_parts.shape[2], up_parts.shape[3])
    down_whole = down_parts.reshape(experts, down_parts.shape[2], down_parts.shape[3])
    gate_owned, up_owned, down_owned = (
        lax.psum_scatter(gate_whole, "dp", scatter_dimension=1, tiled=True),
        lax.psum_scatter(up_whole, "dp", scatter_dimension=1, tiled=True),
        lax.psum_scatter(down_whole, "dp", scatter_dimension=2, tiled=True),
    )
    gate_up_grad = jnp.stack([gate_owned, up_owned])
    down_grad = down_owned
    gate_grad_rows = gate_slots.reshape(-1)[flat_index].reshape(group_rows, top_count)
    mixed_own, expert_part, gate_grad_own = (
        lax.psum_scatter(mixed_sum[:group_rows], "tensor", scatter_dimension=0, tiled=True),
        lax.psum_scatter(row_grads[:group_rows], "tensor", scatter_dimension=0, tiled=True),
        lax.psum_scatter(gate_grad_rows, "tensor", scatter_dimension=0, tiled=True),
    )
    result = hidden + mixed_own
    gates_own = lax.dynamic_slice_in_dim(gate_weights, offset, local_rows, 0)
    chosen_own = lax.dynamic_slice_in_dim(chosen, offset, local_rows, 0)
    select_back = gates_own * (
        gate_grad_own - jnp.sum(gates_own * gate_grad_own, -1, keepdims=True)
    )
    logit_back = jnp.sum(chosen_own * select_back[:, :, None], 1)
    router_part = jnp.dot(normed_two.astype(jnp.float32).T, logit_back, precision=HIGH)
    normed_two_back = expert_part + jnp.dot(
        logit_back, router_low.astype(jnp.float32).T, precision=HIGH
    )
    unit_two = hidden * scale_two
    weighted_two = normed_two_back * norm_gains[1]
    hidden_back = cotangent + scale_two * (
        weighted_two - unit_two * jnp.mean(weighted_two * unit_two, -1, keepdims=True)
    )
    gain_part_two = jnp.sum(normed_two_back * unit_two, 0)
    attention_back = lax.all_gather(hidden_back.astype(jnp.bfloat16), "tensor", axis=0, tiled=True)
    output_grad = jnp.einsum(
        "tf,td->fd", attended, attention_back, preferred_element_type=jnp.float32
    )
    attended_back = jnp.einsum(
        "td,fd->tf", attention_back, output_full, preferred_element_type=jnp.float32
    )
    attended_back = attended_back.astype(jnp.bfloat16).reshape(
        group_rows, pair_heads, share_count, HD
    )
    key_grad = jnp.zeros((group_rows, pair_heads, HD), jnp.float32)
    value_grad = jnp.zeros((group_rows, pair_heads, HD), jnp.float32)
    query_blocks = []
    for block_index in range(block_total):
        row_start = block_index * block_rows
        scores, query_block = block_scores(row_start)
        probabilities = jnp.exp(scores - log_totals[block_index])
        back_block = attended_back[row_start : row_start + block_rows]
        prob_back = jnp.einsum(
            "qkgd,tkd->kgqt", back_block, value_rows, preferred_element_type=jnp.float32
        )
        inner_sum = jnp.sum(probabilities * prob_back, -1, keepdims=True)
        score_back = (probabilities * (prob_back - inner_sum)).astype(jnp.bfloat16)
        query_blocks.append(
            score_scale
            * jnp.einsum("kgqt,tkd->qkgd", score_back, key_rows, preferred_element_type=jnp.float32)
        )
        key_grad = key_grad + score_scale * jnp.einsum(
            "kgqt,qkgd->tkd", score_back, query_block, preferred_element_type=jnp.float32
        )
        value_grad = value_grad + jnp.einsum(
            "kgqt,qkgd->tkd",
            probabilities.astype(jnp.bfloat16),
            back_block,
            preferred_element_type=jnp.float32,
        )
    query_grad_rows = jnp.concatenate(query_blocks, 0).reshape(group_rows, query_heads, HD)
    query_back = (
        rotate(query_grad_rows, cosine, -sine_part)
        .astype(jnp.bfloat16)
        .reshape(group_rows, query_heads * HD)
    )
    key_back = rotate(key_grad, cosine, -sine_part)
    pair_back = (
        jnp.stack([key_back, value_grad])
        .reshape(2, group_rows, pair_heads * HD)
        .astype(jnp.bfloat16)
    )
    query_grad = jnp.einsum("td,tf->df", rows_one, query_back, preferred_element_type=jnp.float32)
    pair_grad = jnp.einsum("td,ctf->cdf", rows_one, pair_back, preferred_element_type=jnp.float32)
    normed_one_back = lax.psum_scatter(
        jnp.einsum("tf,df->td", query_back, query_full, preferred_element_type=jnp.float32)
        + jnp.einsum("ctf,cdf->td", pair_back, pair_full, preferred_element_type=jnp.float32),
        "tensor",
        scatter_dimension=0,
        tiled=True,
    )
    unit_one = stream * scale_one
    weighted_one = normed_one_back * norm_gains[0]
    stream_grad = hidden_back + scale_one * (
        weighted_one - unit_one * jnp.mean(weighted_one * unit_one, -1, keepdims=True)
    )
    gain_part_one = jnp.sum(normed_one_back * unit_one, 0)
    query_owned, pair_owned, output_owned = (
        lax.psum_scatter(query_grad, "dp", scatter_dimension=0, tiled=True),
        lax.psum_scatter(pair_grad, "dp", scatter_dimension=1, tiled=True),
        lax.psum_scatter(output_grad, "dp", scatter_dimension=1, tiled=True),
    )
    gain_grad, router_grad = lax.psum(
        (jnp.stack([gain_part_one, gain_part_two]), router_part), ("dp", "tensor")
    )
    rate_wide = 2.0 * D ** (-0.5)
    rate_output = 2.0 * max(1, 2 * H * HD // group_rows) ** (-0.5)
    rate_router = 2.0 * (4 * D) ** (-0.5)
    rate_down = 2.0 * (FF // 16) ** (-0.5)
    query_moment_new, query_second_new, query_weight_new = adam_update(
        query_weight, query_owned, query_moment, query_second, rate_wide, WEIGHT_DECAY
    )
    pair_moment_new, pair_second_new, pair_weight_new = adam_update(
        key_value_weight, pair_owned, key_value_moment, key_value_second, rate_wide, WEIGHT_DECAY
    )
    output_moment_new, output_second_new, output_weight_new = adam_update(
        output_weight, output_owned, output_moment, output_second, rate_output, WEIGHT_DECAY
    )
    router_moment_new, router_second_new, router_weight_new = adam_update(
        router_weight, router_grad, router_moment, router_second, rate_router, WEIGHT_DECAY
    )
    gate_up_moment_new, gate_up_second_new, gate_up_weight_new = adam_update(
        gate_up_weight, gate_up_grad, gate_up_moment, gate_up_second, rate_wide, WEIGHT_DECAY
    )
    down_moment_new, down_second_new, down_weight_new = adam_update(
        down_weight, down_grad, down_moment, down_second, rate_down, WEIGHT_DECAY
    )
    gains_moment_new, gains_second_new, gains_new = adam_update(
        norm_gains, gain_grad, gains_moment, gains_second, 0.2, 0.0
    )
    return (
        result,
        stream_grad,
        query_moment_new,
        query_second_new,
        query_weight_new,
        pair_moment_new,
        pair_second_new,
        pair_weight_new,
        output_moment_new,
        output_second_new,
        output_weight_new,
        router_moment_new,
        router_second_new,
        router_weight_new,
        gate_up_moment_new,
        gate_up_second_new,
        gate_up_weight_new,
        down_moment_new,
        down_second_new,
        down_weight_new,
        gains_moment_new,
        gains_second_new,
        gains_new,
    )


def solution(mesh):
    placed = (
        P(("dp", "tensor"), None),
        P(("dp", "tensor"), None),
        P("dp", None),
        P("dp", None),
        P("dp", "tensor"),
        P("dp", "tensor"),
        P("dp", "tensor"),
        P(None, "dp", "tensor"),
        P(None, "dp", "tensor"),
        P(None, "dp", "tensor"),
        P("tensor", "dp"),
        P("tensor", "dp"),
        P("tensor", "dp"),
        P(),
        P(),
        P(),
        P(None, None, "dp", "tensor"),
        P(None, None, "dp", "tensor"),
        P(None, None, "dp", "tensor"),
        P(None, "tensor", "dp"),
        P(None, "tensor", "dp"),
        P(None, "tensor", "dp"),
        P(),
        P(),
        P(),
    )
    return jax.shard_map(
        body,
        mesh=mesh,
        in_specs=placed,
        out_specs=(
            P(("dp", "tensor"), None),
            P(("dp", "tensor"), None),
            P("dp", "tensor"),
            P("dp", "tensor"),
            P("dp", "tensor"),
            P(None, "dp", "tensor"),
            P(None, "dp", "tensor"),
            P(None, "dp", "tensor"),
            P("tensor", "dp"),
            P("tensor", "dp"),
            P("tensor", "dp"),
            P(),
            P(),
            P(),
            P(None, None, "dp", "tensor"),
            P(None, None, "dp", "tensor"),
            P(None, None, "dp", "tensor"),
            P(None, "tensor", "dp"),
            P(None, "tensor", "dp"),
            P(None, "tensor", "dp"),
            P(),
            P(),
            P(),
        ),
        check_vma=False,
    )
```

profile of v0, /device:TPU:0, one launch (start us, length us, event | category | flops | bytes accessed | tf_op | source)
XLA Modules:
  0.0 2880.9 jit_solution(7444093251139652822)
XLA Ops:
  16.8 33.2 %all_gather.29 = bf16[1024,256]{1,0:T(8,128)(2,1)S(1)} all-gather(bf16[128,256]{1,0:T(8,128)(2,1)S(1)} %convert_element_type.124), channel_id=1, replica_groups=mesh['dp'=8,'tensor'=4] {'dp'}, dimensions={0}, use_global_device_ids=true | all-gather | bytes 589824 | tf_op jit(solution)/shard_map/all_gather | solution.py:130
  50.0 27.0 all_gather.28
  77.1 27.6 all_gather.30
  128.7 39.6 %reduce-scatter.12.cloned.1.call-done = f32[256,1024]{1,0:T(8,128)} async-done(((f32[1024,1024]{1,0:T(8,128)}), f32[256,1024]{1,0:T(8,128)}) %reduce-scatter.12.cloned.1.call-update) | async-done | bytes 1048592 | tf_op jit(solution)/shard_map/reduce_scatter | solution.py:184
  190.8 30.5 %scatter_custom_fusion.2 = s32[16384]{0:T(1024)S(1)} fusion(s32[8192]{0:T(1024)S(1)} %bitcast.323, s32[8192]{0:T(1024)S(1)} %add_select_fusion, s32[]{:T(128)} %constant.96.clone.1), kind=kCustom, calls=%fused_computation.169 | custom fusion | bytes 65540 | tf_op jit(solution)/shard_map/scatter | solution.py:68
  226.8 30.5 %scatter_custom_fusion.3 = f32[16384]{0:T(1024)S(1)} fusion(s32[8192]{0:T(1024)S(1)} %bitcast.325, f32[8192]{0:T(1024)S(1)} %reshape.381, f32[]{:T(128)} %constant.83.clone.1), kind=kCustom, calls=%fused_computation.167 | custom fusion | bytes 65540 | tf_op jit(solution)/shard_map/scatter | solution.py:205
  260.3 85.7 %all-gather.13.cloned.1.call-done = bf16[32,128,1024]{2,1,0:T(8,128)(2,1)} async-done(((bf16[32,128,128]{2,1,0:T(8,128)(2,1)}), bf16[32,128,1024]{2,1,0:T(8,128)(2,1)}) %all-gather.13.cloned.1.call-update) | async-done | bytes 8388624 | tf_op jit(solution)/shard_map/all_gather | solution.py:262
  346.0 228.7 %all-gather.11.cloned.1.call-done = bf16[2,32,1024,128]{3,2,1,0:T(8,128)(2,1)} async-done(((bf16[2,32,128,128]{3,2,1,0:T(8,128)(2,1)}), bf16[2,32,1024,128]{3,2,1,0:T(8,128)(2,1)}) %all-gather.11.cloned.1.call-update) | async-done | bytes 16777232 | tf_op jit(solution)/shard_map/all_gather | solution.py:261
  579.8 868.3 %while.22 = (s32[]{:T(128)}, f32[1025,1024]{1,0:T(8,128)}, f32[1025,1024]{1,0:T(8,128)}, f32[8,4,1024,128]{3,2,1,0:T(8,128)}, f32[8,4,1024,128]{3,2,1,0:T(8,128)...) while((s32[]{:T(128)}, f32[1025,1024]{1,0:T(8,128)}, ...), condition=%wide.region_22.23_spmd, body=%wide.region_18.22_spmd.sunk | while | flops 4863039488 | bytes 206186480 | solution.py:270
  625.9 23.2 scatter_fusion.1
  665.3 23.1 scatter_fusion
  734.3 23.2 scatter_fusion.1
  842.7 23.2 scatter_fusion.1
  951.2 23.2 scatter_fusion.1
  990.7 23.1 scatter_fusion
  1059.8 23.2 scatter_fusion.1
  1099.2 23.1 scatter_fusion
  1168.2 23.2 scatter_fusion.1
  1276.8 23.2 scatter_fusion.1
  1385.2 23.2 scatter_fusion.1
  1448.1 45.5 %gather_fusion.2 = f32[8192]{0:T(1024)S(1)} fusion(f32[16384]{0:T(1024)S(1)} %bitcast.278, s32[8192]{0:T(1024)S(1)} %copy-done.60), kind=kCustom, calls=%fused_computation.2 | custom fusion | bytes 98304 | tf_op jit(solution)/shard_map/gather | solution.py:283
  1513.9 46.2 %reduce-scatter.16.cloned.1.call-done = f32[256,1024]{1,0:T(8,128)} async-done(((f32[1024,1024]{1,0:T(8,128)}), f32[256,1024]{1,0:T(8,128)}) %reduce-scatter.16.cloned.1.call-update) | async-done | bytes 1048592 | tf_op jit(solution)/shard_map/reduce_scatter | solution.py:286
  1562.9 45.0 %reduce-scatter.14.cloned.1.call-done = f32[256,1024]{1,0:T(8,128)} async-done(((f32[1024,1024]{1,0:T(8,128)}), f32[256,1024]{1,0:T(8,128)}) %reduce-scatter.14.cloned.1.call-update) | async-done | bytes 1048592 | tf_op jit(solution)/shard_map/reduce_scatter | solution.py:285
  1702.0 60.7 %all-reduce.4.cloned.1.call-done = f32[1024,32]{0,1:T(8,128)} async-done(((f32[1024,32]{0,1:T(8,128)}), f32[1024,32]{0,1:T(8,128)}) %all-reduce.4.cloned.1.call-update) | async-done | bytes 131088 | tf_op jit(solution)/shard_map/psum | solution.py:374
  1764.5 65.0 %reduce-scatter.24.cloned.1.call-done = f32[2,128,128]{1,2,0:T(8,128)} async-done(((f32[2,1024,128]{1,2,0:T(8,128)}), f32[2,128,128]{1,2,0:T(8,128)}) %reduce-scatter.24.cloned.1.call-update) | async-done | bytes 131088 | tf_op jit(solution)/shard_map/reduce_scatter | solution.py:371
  1832.8 63.5 %reduce-scatter.22.cloned.1.call-done = f32[128,256]{1,0:T(8,128)} async-done(((f32[1024,256]{1,0:T(8,128)}), f32[128,256]{1,0:T(8,128)}) %reduce-scatter.22.cloned.1.call-update) | async-done | bytes 131088 | tf_op jit(solution)/shard_map/reduce_scatter | solution.py:370
  1898.0 65.1 %reduce-scatter.26.cloned.1.call-done = f32[256,128]{1,0:T(8,128)} async-done(((f32[256,1024]{1,0:T(8,128)}), f32[256,128]{1,0:T(8,128)}) %reduce-scatter.26.cloned.1.call-update) | async-done | bytes 131088 | tf_op jit(solution)/shard_map/reduce_scatter | solution.py:372
  1964.9 44.8 %reduce-scatter.20.cloned.1.call-done = f32[256,1024]{1,0:T(8,128)} async-done(((f32[1024,1024]{1,0:T(8,128)}), f32[256,1024]{1,0:T(8,128)}) %reduce-scatter.20.cloned.1.call-update) | async-done | bytes 1048592 | tf_op jit(solution)/shard_map/reduce_scatter | solution.py:356
  2011.4 43.2 %psum.15 = f32[2,1024]{1,0:T(2,128)S(1)} all-reduce(f32[2,1024]{1,0:T(2,128)S(1)} %pad_maximum_fusion.9), channel_id=1, replica_groups=mesh['dp'=8,'tensor'=4] {'dp','tensor'}, use_global_device_ids=true, to_apply=%region_42.43 | all-reduce | flops 2048 | bytes 16384 | tf_op jit(solution)/shard_map/psum | solution.py:374
  2057.7 238.7 %reduce-scatter.28.cloned.1.call-done = f32[32,128,128]{2,1,0:T(8,128)} async-done(((f32[32,1024,128]{2,1,0:T(8,128)}), f32[32,128,128]{2,1,0:T(8,128)}) %reduce-scatter.28.cloned.1.call-update) | async-done | bytes 2097168 | tf_op jit(solution)/shard_map/reduce_scatter | solution.py:277
  2296.5 285.1 %reduce-scatter.30.cloned.1.call-done = f32[32,128,128]{2,1,0:T(8,128)} async-done(((f32[32,1024,128]{2,1,0:T(8,128)}), f32[32,128,128]{2,1,0:T(8,128)}) %reduce-scatter.30.cloned.1.call-update) | async-done | bytes 2097168 | tf_op jit(solution)/shard_map/reduce_scatter | solution.py:278
  2591.9 275.1 %reduce-scatter.32.cloned.1.call-done = f32[32,128,128]{2,1,0:T(8,128)} async-done(((f32[32,128,1024]{2,1,0:T(8,128)}), f32[32,128,128]{2,1,0:T(8,128)}) %reduce-scatter.32.cloned.1.call-update) | async-done | bytes 2097168 | tf_op jit(solution)/shard_map/reduce_scatter | solution.py:279
  (535 shorter events, 818.3 us)
Async XLA Ops:
  7.2 99.7 %all-gather.7.cloned.1.call-start = ((), (), s32[]{:S(2)}) async-start(), calls=%async_computation.11 | async-start | bytes 2621440 | tf_op jit(solution)/shard_map/all_gather | solution.py:136
  12.2 156.2 %reduce-scatter.12.cloned.1.call-start = ((), (), s32[]{:S(2)}) async-start(), calls=%async_computation.12 | async-start | bytes 5242880 | tf_op jit(solution)/shard_map/reduce_scatter | solution.py:184
  126.4 95.6 %all-gather.15.cloned.1.call-start = ((), (), s32[]{:S(2)}) async-start(), calls=%async_computation.16 | async-start | bytes 2621440 | tf_op jit(solution)/shard_map/all_gather | solution.py:195
  128.7 95.0 %all-gather.9.cloned.1.call-start = ((), (), s32[]{:S(2)}) async-start(), calls=%async_computation.13 | async-start | bytes 2621440 | tf_op jit(solution)/shard_map/all_gather | solution.py:194
  171.7 174.3 %all-gather.13.cloned.1.call-start = ((), (), s32[]{:S(2)}) async-start(), calls=%async_computation.15 | async-start | bytes 9437184 | tf_op jit(solution)/shard_map/all_gather | solution.py:262
  173.0 401.7 %all-gather.11.cloned.1.call-start = ((), (), s32[]{:S(2)}) async-start(), calls=%async_computation.14 | async-start | bytes 18874368 | tf_op jit(solution)/shard_map/all_gather | solution.py:261
  176.9 1335.5 %reduce-scatter.18.cloned.1.call-start = ((), (), s32[]{:S(2)}) async-start(), calls=%async_computation.19 | async-start | bytes 40960 | tf_op jit(solution)/shard_map/reduce_scatter | solution.py:287
  226.3 350.9 %copy-start.52 = (f32[1024,8]{0,1:T(8,128)}, f32[1024,8]{0,1:T(8,128)S(1)}, u32[]{:S(2)}) copy-start(f32[1024,8]{0,1:T(8,128)S(1)} %fusion.69) | copy-start | bytes 98308
  579.8 868.4 %copy-start.60 = (s32[8192]{0:T(1024)S(1)}, s32[8192]{0:T(1024)}, u32[]{:S(2)}) copy-start(s32[8192]{0:T(1024)} %broadcast_clamp_fusion.1) | copy-start | bytes 98308
  1494.8 65.3 %reduce-scatter.16.cloned.1.call-start = ((), (), s32[]{:S(2)}) async-start(), calls=%async_computation.18 | async-start | bytes 5242880 | tf_op jit(solution)/shard_map/reduce_scatter | solution.py:286
  1499.6 108.3 %reduce-scatter.14.cloned.1.call-start = ((), (), s32[]{:S(2)}) async-start(), calls=%async_computation.17 | async-start | bytes 5242880 | tf_op jit(solution)/shard_map/reduce_scatter | solution.py:285
  1504.6 129.5 %all-gather.17.cloned.1.call-start = ((), (), s32[]{:S(2)}) async-start(), calls=%async_computation.20 | async-start | bytes 2621440 | tf_op jit(solution)/shard_map/all_gather | solution.py:306
  1611.3 151.4 %all-reduce.4.cloned.1.call-start = ((), (), s32[]{:S(2)}) async-start(), calls=%async_computation.25 | async-start | bytes 262144 | tf_op jit(solution)/shard_map/psum | solution.py:374
  1612.4 217.1 %reduce-scatter.24.cloned.1.call-start = ((), (), s32[]{:S(2)}) async-start(), calls=%async_computation.23 | async-start | bytes 1179648 | tf_op jit(solution)/shard_map/reduce_scatter | solution.py:371
  1684.9 211.4 %reduce-scatter.22.cloned.1.call-start = ((), (), s32[]{:S(2)}) async-start(), calls=%async_computation.22 | async-start | bytes 1179648 | tf_op jit(solution)/shard_map/reduce_scatter | solution.py:370
  1692.6 270.5 %reduce-scatter.26.cloned.1.call-start = ((), (), s32[]{:S(2)}) async-start(), calls=%async_computation.24 | async-start | bytes 1179648 | tf_op jit(solution)/shard_map/reduce_scatter | solution.py:372
  1696.0 313.7 %reduce-scatter.20.cloned.1.call-start = ((), (), s32[]{:S(2)}) async-start(), calls=%async_computation.21 | async-start | bytes 5242880 | tf_op jit(solution)/shard_map/reduce_scatter | solution.py:356
  1699.7 596.8 %reduce-scatter.28.cloned.1.call-start = ((), (), s32[]{:S(2)}) async-start(), calls=%async_computation.26 | async-start | bytes 18874368 | tf_op jit(solution)/shard_map/reduce_scatter | solution.py:277
  1700.2 881.3 %reduce-scatter.30.cloned.1.call-start = ((), (), s32[]{:S(2)}) async-start(), calls=%async_computation.27 | async-start | bytes 18874368 | tf_op jit(solution)/shard_map/reduce_scatter | solution.py:278
  1700.8 1166.2 %reduce-scatter.32.cloned.1.call-start = ((), (), s32[]{:S(2)}) async-start(), calls=%async_computation.28 | async-start | bytes 18874368 | tf_op jit(solution)/shard_map/reduce_scatter | solution.py:279
  1700.9 195.3 %copy-start.48 = (f32[128,256]{1,0:T(8,128)S(1)}, f32[128,256]{1,0:T(8,128)}, u32[]{:S(2)}) copy-start(f32[128,256]{1,0:T(8,128)} %param.31) | copy-start | bytes 393220
  1701.0 195.3 %copy-start.56 = (f32[128,256]{1,0:T(8,128)S(1)}, f32[128,256]{1,0:T(8,128)}, u32[]{:S(2)}) copy-start(f32[128,256]{1,0:T(8,128)} %param.33) | copy-start | bytes 393220
  1701.0 262.1 %copy-start.49 = (f32[256,128]{1,0:T(8,128)S(1)}, f32[256,128]{1,0:T(8,128)}, u32[]{:S(2)}) copy-start(f32[256,128]{1,0:T(8,128)} %param.37) | copy-start | bytes 393220
  1701.8 308.0 %copy-start.12 = (f32[256,1024]{1,0:T(8,128)S(1)}, f32[256,1024]{1,0:T(8,128)}, u32[]{:S(2)}) copy-start(f32[256,1024]{1,0:T(8,128)} %param.27) | copy-start | bytes 3145732
  1701.8 308.0 %copy-start.66 = (f32[1,1024]{1,0:T(1,128)S(1)}, f32[1,1024]{1,0:T(1,128)}, u32[]{:S(2)}) copy-start(f32[1,1024]{1,0:T(1,128)} %copy-done.65) | copy-start | bytes 12292
  1701.8 308.0 %copy-start.71 = (f32[256]{0:T(256)S(1)}, f32[256]{0:T(256)}, u32[]{:S(2)}) copy-start(f32[256]{0:T(256)} %copy-done.70) | copy-start | bytes 3076
  1701.8 352.8 %copy-start.69 = (f32[2,1024]{1,0:T(2,128)S(1)}, f32[2,1024]{1,0:T(2,128)}, u32[]{:S(2)}) copy-start(f32[2,1024]{1,0:T(2,128)} %param.49) | copy-start | bytes 24580
  1701.8 353.5 %copy-start.28 = (f32[256,1024]{1,0:T(8,128)S(1)}, f32[256,1024]{1,0:T(8,128)}, u32[]{:S(2)}) copy-start(f32[256,1024]{1,0:T(8,128)} %get-tuple-element.332) | copy-start | bytes 3145732
  1764.5 246.9 %copy-start.72 = (f32[1024]{0:T(1024)S(1)}, f32[1024]{0:T(1024)}, u32[]{:S(2)}) copy-start(f32[1024]{0:T(1024)} %get-tuple-element.278) | copy-start | bytes 12292
  1764.5 290.1 %copy-start.75 = (f32[2,1024]{1,0:T(2,128)S(1)}, f32[2,1024]{1,0:T(2,128)}, u32[]{:S(2)}) copy-start(f32[2,1024]{1,0:T(2,128)} %param.51) | copy-start | bytes 24580
  1764.5 290.1 %copy-start.76 = (f32[2,1024]{1,0:T(2,128)S(1)}, f32[2,1024]{1,0:T(2,128)}, u32[]{:S(2)}) copy-start(f32[2,1024]{1,0:T(2,128)} %param.50) | copy-start | bytes 24580
  2581.5 285.5 %copy-start.20 = (f32[32,128,128]{2,1,0:T(8,128)S(1)}, f32[32,128,128]{2,1,0:T(8,128)}, u32[]{:S(2)}) copy-start(f32[32,128,128]{2,1,0:T(8,128)} %param.46) | copy-start | bytes 6291460
  (102 other events, 1663.7 us)
Sparse Core Ops, SparseCore 0:
  12.3 25.2 all-gather.6
  126.5 41.8 reduce-scatter.11
  170.6 22.5 all-gather.14
  195.3 22.5 all-gather.8
  220.6 125.3 all-gather.12
  348.9 225.7 all-gather.10
  1494.9 17.5 reduce-scatter.17
  1515.6 44.4 reduce-scatter.15
  1563.4 44.5 reduce-scatter.13
  1611.5 22.5 all-gather.16
  1640.2 122.5 all-reduce.3
  1766.6 62.8 reduce-scatter.23
  1833.8 62.3 reduce-scatter.21
  1900.1 62.9 reduce-scatter.25
  1966.2 43.4 reduce-scatter.19
  2013.4 283.0 reduce-scatter.27
  2300.6 280.9 reduce-scatter.29
  2585.2 281.7 reduce-scatter.31
where the time goes:
time: 2890 us; the launch traced here: 2880 us
  waiting for transfers between devices  1570 us (54%)
  other arithmetic  454 us (16%)
  matrix products  370 us (13%)
  local copies, waits for them, and re-layouts  324 us (11%)
  blocking collectives  131 us (5%)
    reduce_scatter x1, waiting for transfers between devices, body(): lax.psum_scatter(up_whole, 'dp', scatter_dimension=1, tiled=True)  285 us
    reduce_scatter x1, waiting for transfers between devices, body(): lax.psum_scatter(down_whole, 'dp', scatter_dimension=2, tiled=True)  275 us
    reduce_scatter x1, waiting for transfers between devices, body(): lax.psum_scatter(gate_whole, 'dp', scatter_dimension=1, tiled=True)  239 us
    all_gather x1, waiting for transfers between devices, body(): lax.all_gather(gate_up_weight.astype(jnp.bfloat16), 'dp', axis=2, tiled=T...  229 us
    scatter-add x8, other arithmetic, expert_work(): row_grads.at[slots_here].add(slot_back.reshape(together * capacity, D))  185 us
    scatter-add x8, other arithmetic, expert_work(): mixed_sum.at[slots_here]  185 us
    gather x8, local copies, waits for them, and re-layouts, expert_work(): inputs_here = padded_rows[slots_here].reshape(together, capacity, D)  102 us
    all_gather x1, waiting for transfers between devices, body(): lax.all_gather(down_weight.astype(jnp.bfloat16), 'dp', axis=2, tiled=True)  85.7 us
  transfers between devices with their start and end apart: 18, of which 15 were waited for; matrix products, arithmetic and copies ran while one was open for 7% of the time, Pallas kernels for 0%

commit v1 on v0

v1 whole, which is shorter than its diff:
```python
import jax
import jax.numpy as jnp
from jax import lax
from jax.experimental import pallas as pl
from jax.experimental.pallas import tpu as pltpu
from jax.sharding import Mesh
from jax.sharding import PartitionSpec as P

D = 1024
H = 16
HD = 64
FF = 512
STEP = 10


EPS = 1e-05
HIGH = lax.Precision.HIGHEST
BETA_ONE = 0.9
BETA_TWO = 0.95
WEIGHT_DECAY = 0.1
LANES = 128
BF = jnp.bfloat16
F32 = jnp.float32
Z, Y, X, C = 4, 2, 2, 2
EVERY = ("blk", "z", "y", "x", "core")
DATA = ("blk", "z", "y")


def positions(length_row, row_index):
    end_points = jnp.cumsum(length_row)
    start_points = end_points - length_row
    segment = jnp.sum((row_index[:, None] >= end_points[None, :]).astype(jnp.int32), 1)
    member = segment[:, None] == jnp.arange(length_row.shape[0], dtype=jnp.int32)[None, :]
    position = row_index - jnp.sum(jnp.where(member, start_points[None, :], 0), 1)
    return (segment, position)


def rope_tables(position, half_size):
    frequency = 10000.0 ** (-jnp.arange(half_size, dtype=jnp.float32) / half_size)
    angles = position.astype(jnp.float32)[:, None] * frequency[None, :]
    return (jnp.cos(angles), jnp.sin(angles))


def rotate(vectors, cosine, sine_part):
    half_size = vectors.shape[-1] // 2
    first_half = vectors[..., :half_size]
    second_half = vectors[..., half_size:]
    cosine_rows = cosine[:, None, :]
    sine_rows = sine_part[:, None, :]
    return jnp.concatenate(
        [
            first_half * cosine_rows - second_half * sine_rows,
            second_half * cosine_rows + first_half * sine_rows,
        ],
        -1,
    )


def adam_update(weight, gradient, moment, second, step_rate, decay_rate):
    new_moment = BETA_ONE * moment + (1.0 - BETA_ONE) * gradient
    new_second = BETA_TWO * second + (1.0 - BETA_TWO) * gradient * gradient
    moment_hat = new_moment / (1.0 - BETA_ONE**STEP)
    second_hat = new_second / (1.0 - BETA_TWO**STEP)
    new_weight = weight - step_rate * (
        moment_hat / (jnp.sqrt(second_hat) + 1e-08) + decay_rate * weight
    )
    return (new_moment, new_second, new_weight)


def partner(value, axis, mask=1):
    size = lax.axis_size(axis)
    return lax.ppermute(value, axis, [(i, i ^ mask) for i in range(size)])


def to_absolute(stacked, axis, dim):
    place = lax.axis_index(axis)
    bit = 1
    while bit < stacked.shape[dim]:
        order = [k ^ bit for k in range(stacked.shape[dim])]
        parts = [lax.slice_in_dim(stacked, k, k + 1, axis=dim) for k in order]
        other = jnp.concatenate(parts, dim)
        stacked = jnp.where((place & bit) != 0, other, stacked)
        bit *= 2
    return stacked


def pick(value, index, dim):
    return lax.dynamic_index_in_dim(value, index, dim, keepdims=False)


def gather_tensor(own):
    across = partner(own, "x")
    beside = partner(own, "core")
    return [own, beside, across, partner(across, "core")]


def scatter_tensor(blocks):
    sent = jnp.stack([blocks[1], blocks[3]]).astype(BF)
    got = partner(sent, "core").astype(F32)
    mine = blocks[0] + got[0]
    theirs = (blocks[2] + got[1]).astype(BF)
    return mine + partner(theirs, "x").astype(F32)


def nt_dot(left, right):
    return lax.dot_general(left, right, (((1,), (1,)), ((), ())), preferred_element_type=F32)


def expert_kernel(base, r0, r1, b0, b1, w, gu, gm, mixed, part, rows, back, acc_m, acc_p, acc_g):
    i = pl.program_id(0)
    half = r0.shape[0]

    @pl.when(i == 0)
    def _():
        rows[:half, :] = r0[...]
        rows[half:, :] = r1[...]
        back[:half, :] = b0[...]
        back[half:, :] = b1[...]
        acc_m[...] = jnp.zeros_like(acc_m)
        acc_p[...] = jnp.zeros_like(acc_p)
        acc_g[...] = jnp.zeros_like(acc_g)

    expert = base[0] + i
    mine = rows[:, :D]
    gate_lanes = rows[:, D:].astype(F32)
    lane = lax.broadcasted_iota(jnp.int32, gate_lanes.shape, 1)
    wanted = (lane == expert) | (lane == expert + 32)
    gate = jnp.sum(jnp.where(wanted, gate_lanes, 0.0), 1, keepdims=True)
    wg = w[0, :, :FF]
    wu = w[0, :, FF : 2 * FF]
    wd = w[0, :, 2 * FF :]
    gate_pre = jnp.dot(mine, wg, preferred_element_type=F32)
    up_pre = jnp.dot(mine, wu, preferred_element_type=F32)
    raw_back = jnp.dot(back[...], wd, preferred_element_type=F32)
    sig = jax.nn.sigmoid(gate_pre)
    active = gate_pre * sig
    middle = (active * up_pre).astype(BF).astype(F32)
    gate_grad = jnp.sum(middle * raw_back, 1, keepdims=True)
    acc_g[...] += jnp.where(lane == expert, gate_grad, 0.0)
    scaled = (gate * middle).astype(BF)
    middle_back = gate * raw_back
    gate_back = (middle_back * up_pre * sig * (1.0 + gate_pre * (1.0 - sig))).astype(BF)
    up_back = (middle_back * active).astype(BF)
    gu[:, :FF] = gate_back
    gu[:, FF:] = up_back
    gm[...] = scaled
    acc_m[...] += nt_dot(scaled, wd)
    acc_p[...] += nt_dot(gate_back, wg) + nt_dot(up_back, wu)

    @pl.when(i == pl.num_programs(0) - 1)
    def _():
        mixed[...] = acc_m[...].astype(BF)
        part[:, :D] = acc_p[...].astype(BF)
        part[:, D:] = acc_g[...].astype(BF)


def expert_chunk(base, r0, r1, b0, b1, weights):
    together = weights.shape[0]
    half, wide = r0.shape
    count = 2 * half
    whole = lambda i, s: (0, 0)
    return pl.pallas_call(
        expert_kernel,
        grid_spec=pltpu.PrefetchScalarGridSpec(
            num_scalar_prefetch=1,
            grid=(together,),
            in_specs=[
                pl.BlockSpec((half, wide), whole),
                pl.BlockSpec((half, wide), whole),
                pl.BlockSpec((half, D), whole),
                pl.BlockSpec((half, D), whole),
                pl.BlockSpec((1, D, 3 * FF), lambda i, s: (i, 0, 0)),
            ],
            out_specs=[
                pl.BlockSpec((count, 2 * FF), lambda i, s: (0, i)),
                pl.BlockSpec((count, FF), lambda i, s: (0, i)),
                pl.BlockSpec((count, D), whole),
                pl.BlockSpec((count, wide), whole),
            ],
            scratch_shapes=[
                pltpu.VMEM((count, wide), BF),
                pltpu.VMEM((count, D), BF),
                pltpu.VMEM((count, D), F32),
                pltpu.VMEM((count, D), F32),
                pltpu.VMEM((count, LANES), F32),
            ],
        ),
        out_shape=[
            jax.ShapeDtypeStruct((count, together * 2 * FF), BF),
            jax.ShapeDtypeStruct((count, together * FF), BF),
            jax.ShapeDtypeStruct((count, D), BF),
            jax.ShapeDtypeStruct((count, wide), BF),
        ],
        compiler_params=pltpu.CompilerParams(vmem_limit_bytes=48 * 1024 * 1024),
        cost_estimate=pl.CostEstimate(
            flops=12 * together * count * D * FF,
            bytes_accessed=6 * together * D * FF + 16 * count * D,
            transcendentals=together * count * FF,
        ),
        name="experts",
    )(base, r0, r1, b0, b1, weights)


def body(
    stream,
    cotangent,
    lengths,
    routes,
    query_weight,
    query_moment,
    query_second,
    key_value_weight,
    key_value_moment,
    key_value_second,
    output_weight,
    output_moment,
    output_second,
    router_weight,
    router_moment,
    router_second,
    gate_up_weight,
    gate_up_moment,
    gate_up_second,
    down_weight,
    down_moment,
    down_second,
    norm_gains,
    gains_moment,
    gains_second,
):
    blocks = lax.axis_size("blk")
    z, y, x, c = (lax.axis_index(a) for a in ("z", "y", "x", "core"))
    place = x * C + c
    local_rows = stream.shape[0]
    group_rows = local_rows * X * C
    experts = down_weight.shape[0]
    depth = query_weight.shape[0]
    deep = depth * blocks
    block_rows = min(512, group_rows)
    block_total = group_rows // block_rows
    query_wide = query_weight.shape[1]
    pair_wide = key_value_weight.shape[2]
    query_heads = query_wide // HD
    pair_heads = pair_wide // HD
    share_count = query_heads // pair_heads
    score_scale = HD ** (-0.5)
    together = experts // (Z * C)
    row_index = jnp.concatenate(
        [(place ^ b) * local_rows + jnp.arange(local_rows, dtype=jnp.int32) for b in range(X * C)]
    )
    segment, position = positions(lengths[0], row_index)
    cosine, sine_part = rope_tables(position, HD // 2)

    attn_own = jnp.concatenate(
        [query_weight, key_value_weight[0], key_value_weight[1], output_weight.T], 1
    ).astype(BF)
    if blocks > 1:
        attn_own = lax.all_gather(attn_own, "blk", axis=0, tiled=True)
    attn_z = jnp.stack([attn_own] + [partner(attn_own, "z", s) for s in range(1, Z)])
    attn_y = jnp.stack([attn_z, partner(attn_z, "y")], 1)
    attn_all = to_absolute(to_absolute(attn_y, "y", 1), "z", 0)
    attn_wide = attn_own.shape[1]
    if blocks > 1:
        attn_all = attn_all.reshape(Z, Y, blocks, depth, attn_wide).transpose(2, 0, 1, 3, 4)
    attn_all = attn_all.reshape(D, attn_wide)
    first_pair = query_wide + pair_wide
    second_pair = first_pair + pair_wide
    qkv_full = attn_all[:, :second_pair]
    output_full = attn_all[:, second_pair:]

    scale_one = lax.rsqrt(jnp.mean(stream * stream, -1, keepdims=True) + EPS)
    normed_one = (stream * scale_one * norm_gains[0]).astype(BF)
    rows_one = jnp.concatenate(gather_tensor(normed_one), 0)

    back_own = cotangent.astype(BF)
    back_z = [back_own] + [partner(back_own, "z", s) for s in range(1, Z)]
    back_pairs = [(v, partner(v, "core")) for v in back_z]

    expert_own = jnp.concatenate(
        [gate_up_weight[0], gate_up_weight[1], down_weight.transpose(0, 2, 1)], 2
    ).astype(BF)
    expert_wide = expert_own.shape[2]
    if blocks > 1:
        expert_own = lax.all_gather(expert_own, "blk", axis=1, tiled=True)
    expert_own = expert_own.reshape(Z, C, together, deep, expert_wide)
    kept = pick(expert_own, c, 1)
    moved = partner(pick(expert_own, 1 - c, 1), "core")
    both = jnp.stack([kept, moved])
    from_z = [pick(both, z, 1)] + [
        partner(pick(both, z ^ s, 1), "z", s) for s in range(1, Z)
    ]
    pieces = jnp.stack(from_z, 1)
    here = [[None, None], [None, None]]
    piece_a, piece_b = pieces[0], pieces[1]
    a_x = partner(piece_a, "x")
    b_y = partner(piece_b, "y")
    grid_a = jnp.stack(
        [jnp.stack([piece_a, a_x]), jnp.stack([partner(piece_a, "y"), partner(a_x, "y")])]
    )
    grid_b = jnp.stack(
        [jnp.stack([piece_b, partner(piece_b, "x")]), jnp.stack([b_y, partner(b_y, "x")])]
    )
    grid = jnp.stack([grid_a, grid_b], 3).reshape(
        Y, X, Z, C, together, blocks, depth, 3, expert_wide // 3
    )
    grid = to_absolute(to_absolute(grid, "y", 0), "z", 2)
    expert_weights = grid.transpose(4, 5, 2, 0, 6, 7, 1, 3, 8).reshape(together, D, 3 * FF)

    qkv_raw = jnp.dot(rows_one, qkv_full, preferred_element_type=F32)
    queries = (
        rotate(qkv_raw[:, :query_wide].reshape(group_rows, query_heads, HD), cosine, sine_part)
        .astype(BF)
        .reshape(group_rows, pair_heads, share_count, HD)
    )
    key_rows = rotate(
        qkv_raw[:, query_wide:first_pair].reshape(group_rows, pair_heads, HD), cosine, sine_part
    ).astype(BF)
    value_rows = qkv_raw[:, first_pair:].reshape(group_rows, pair_heads, HD).astype(BF)

    def block_scores(row_start):
        query_block = queries[row_start : row_start + block_rows]
        segment_block = segment[row_start : row_start + block_rows]
        index_block = row_index[row_start : row_start + block_rows]
        scores = score_scale * jnp.einsum(
            "qkgd,tkd->kgqt", query_block, key_rows, preferred_element_type=F32
        )
        allowed = (segment_block[:, None] == segment[None, :]) & (
            row_index[None, :] <= index_block[:, None]
        )
        return (jnp.where(allowed, scores, -1e30), query_block)

    log_totals = []
    attended_blocks = []
    for block_index in range(block_total):
        scores, query_block = block_scores(block_index * block_rows)
        maximum = jnp.max(scores, -1, keepdims=True)
        log_total = maximum + jnp.log(jnp.sum(jnp.exp(scores - maximum), -1, keepdims=True))
        probabilities = jnp.exp(scores - log_total)
        attended_blocks.append(
            jnp.einsum(
                "kgqt,tkd->qkgd",
                probabilities.astype(BF),
                value_rows,
                preferred_element_type=F32,
            )
        )
        log_totals.append(log_total)
    attended = jnp.concatenate(attended_blocks, 0).reshape(group_rows, query_heads * HD).astype(BF)
    attention_part = nt_dot(attended, output_full)
    hidden = stream + scatter_tensor(
        [attention_part[b * local_rows : (b + 1) * local_rows] for b in range(X * C)]
    )
    scale_two = lax.rsqrt(jnp.mean(hidden * hidden, -1, keepdims=True) + EPS)
    normed_two = (hidden * scale_two * norm_gains[1]).astype(BF)

    router_low = router_weight.astype(BF)
    logits = jnp.dot(normed_two, router_low, preferred_element_type=F32)
    routes_own = lax.dynamic_slice_in_dim(routes, place * local_rows, local_rows, 0)
    chosen = jnp.any(
        routes_own[:, :, None] == jnp.arange(experts, dtype=jnp.int32)[None, None, :], 1
    )
    masked = jnp.where(chosen, logits, -jnp.inf)
    raised = jnp.exp(masked - jnp.max(masked, -1, keepdims=True))
    gates = raised / jnp.sum(raised, -1, keepdims=True)
    gates_high = gates.astype(BF)
    gates_low = (gates - gates_high.astype(F32)).astype(BF)
    rows_own = jnp.concatenate(
        [
            normed_two,
            gates_high,
            gates_low,
            jnp.zeros((local_rows, LANES - 2 * experts), BF),
        ],
        1,
    )
    rows_z = [rows_own] + [partner(rows_own, "z", s) for s in range(1, Z)]
    rows_pairs = [(v, partner(v, "core")) for v in rows_z]
    base = ((z * C + c) * together).astype(jnp.int32).reshape(1)
    hidden_parts = []
    down_parts = []
    mixed_total = None
    back_total = None
    for s in range(Z):
        gu, gm, mixed, part = expert_chunk(base, *rows_pairs[s], *back_pairs[s], expert_weights)
        hidden_parts.append(gu)
        down_parts.append(gm)
        part_sum = part[:local_rows].astype(F32) + partner(part[local_rows:], "core").astype(F32)
        mixed_sum = mixed[:local_rows].astype(F32) + partner(mixed[local_rows:], "core").astype(F32)
        if s == 0:
            back_total, mixed_total = part_sum, mixed_sum
        else:
            back_total = back_total + partner(part_sum.astype(BF), "z", s).astype(F32)
            mixed_total = mixed_total + partner(mixed_sum.astype(BF), "z", s).astype(F32)
    result = hidden + mixed_total

    rows_all = jnp.concatenate([v[:, :D] for pair in rows_pairs for v in pair], 0)
    back_all = jnp.concatenate([v for pair in back_pairs for v in pair], 0)
    hidden_grad = lax.dot_general(
        rows_all,
        jnp.concatenate(hidden_parts, 0),
        (((0,), (0,)), ((), ())),
        preferred_element_type=F32,
    ).astype(BF)
    down_grad = lax.dot_general(
        back_all,
        jnp.concatenate(down_parts, 0),
        (((0,), (0,)), ((), ())),
        preferred_element_type=F32,
    ).astype(BF)
    lane_wide = expert_wide // 3
    grads = jnp.concatenate(
        [
            hidden_grad.reshape(blocks, Z, Y, depth, together, 2, X, C, lane_wide),
            down_grad.reshape(blocks, Z, Y, depth, together, 1, X, C, lane_wide),
        ],
        5,
    )
    grads = grads.transpose(7, 6, 2, 1, 4, 0, 3, 5, 8).reshape(
        C, X, Y, Z, together, deep, expert_wide
    )
    grads_a, grads_b = grads[0], grads[1]
    keep_a = pick(grads_a, y, 1).astype(F32)
    got_a = partner(pick(grads_a, 1 - y, 1), "y").astype(F32)
    sum_a = keep_a + got_a
    total_a = sum_a[0] + partner(sum_a[1].astype(BF), "x").astype(F32)
    sum_b = grads_b[0].astype(F32) + partner(grads_b[1], "x").astype(F32)
    total_b = pick(sum_b, y, 0) + partner(pick(sum_b, 1 - y, 0).astype(BF), "y").astype(F32)
    totals = jnp.stack([total_a, total_b]).astype(BF)
    owned_z = jnp.stack(
        [pick(totals, z, 1)] + [partner(pick(totals, z ^ s, 1), "z", s) for s in range(1, Z)], 1
    )
    owned = jnp.stack([owned_z[0], partner(owned_z[1], "core")], 1)
    owned = to_absolute(to_absolute(owned, "core", 1), "z", 0)
    owned = owned.reshape(experts, deep, expert_wide)
    if blocks > 1:
        owned = lax.psum_scatter(owned.astype(F32), "blk", scatter_dimension=1, tiled=True)
    owned = owned.reshape(experts, depth, 3, lane_wide).astype(F32)
    gate_up_grad = jnp.stack([owned[:, :, 0], owned[:, :, 1]])
    down_owned = owned[:, :, 2].transpose(0, 2, 1)

    expert_part = back_total[:, :D]
    gate_grad = back_total[:, D : D + experts]
    logit_back = gates * (gate_grad - jnp.sum(gates * gate_grad, -1, keepdims=True))
    router_part = jnp.dot(normed_two.astype(F32).T, logit_back, precision=HIGH)
    normed_two_back = expert_part + jnp.dot(logit_back, router_low.astype(F32).T, precision=HIGH)
    unit_two = hidden * scale_two
    weighted_two = normed_two_back * norm_gains[1]
    hidden_back = cotangent + scale_two * (
        weighted_two - unit_two * jnp.mean(weighted_two * unit_two, -1, keepdims=True)
    )
    gain_part_two = jnp.sum(normed_two_back * unit_two, 0)
    attention_back = jnp.concatenate(gather_tensor(hidden_back.astype(BF)), 0)
    output_grad = lax.dot_general(
        attention_back, attended, (((0,), (0,)), ((), ())), preferred_element_type=F32
    )
    attended_back = jnp.dot(attention_back, output_full, preferred_element_type=F32)
    attended_back = attended_back.astype(BF).reshape(group_rows, pair_heads, share_count, HD)
    key_grad = jnp.zeros((group_rows, pair_heads, HD), F32)
    value_grad = jnp.zeros((group_rows, pair_heads, HD), F32)
    query_blocks = []
    for block_index in range(block_total):
        row_start = block_index * block_rows
        scores, query_block = block_scores(row_start)
        probabilities = jnp.exp(scores - log_totals[block_index])
        back_block = attended_back[row_start : row_start + block_rows]
        prob_back = jnp.einsum(
            "qkgd,tkd->kgqt", back_block, value_rows, preferred_element_type=F32
        )
        inner_sum = jnp.sum(probabilities * prob_back, -1, keepdims=True)
        score_back = (probabilities * (prob_back - inner_sum)).astype(BF)
        query_blocks.append(
            score_scale
            * jnp.einsum("kgqt,tkd->qkgd", score_back, key_rows, preferred_element_type=F32)
        )
        key_grad = key_grad + score_scale * jnp.einsum(
            "kgqt,qkgd->tkd", score_back, query_block, preferred_element_type=F32
        )
        value_grad = value_grad + jnp.einsum(
            "kgqt,qkgd->tkd", probabilities.astype(BF), back_block, preferred_element_type=F32
        )
    query_grad_rows = jnp.concatenate(query_blocks, 0).reshape(group_rows, query_heads, HD)
    query_back = rotate(query_grad_rows, cosine, -sine_part).reshape(group_rows, query_wide)
    key_back = rotate(key_grad, cosine, -sine_part).reshape(group_rows, pair_wide)
    value_back = value_grad.reshape(group_rows, pair_wide)
    qkv_back = jnp.concatenate([query_back, key_back, value_back], 1).astype(BF)
    qkv_grad = lax.dot_general(
        rows_one, qkv_back, (((0,), (0,)), ((), ())), preferred_element_type=F32
    )
    normed_part = nt_dot(qkv_back, qkv_full)
    normed_one_back = scatter_tensor(
        [normed_part[b * local_rows : (b + 1) * local_rows] for b in range(X * C)]
    )
    unit_one = stream * scale_one
    weighted_one = normed_one_back * norm_gains[0]
    stream_grad = hidden_back + scale_one * (
        weighted_one - unit_one * jnp.mean(weighted_one * unit_one, -1, keepdims=True)
    )
    gain_one = jnp.sum(normed_one_back * unit_one, 0)

    def data_scatter(grad):
        wide = grad.shape[1]
        grad = grad.reshape(blocks, Z, Y, depth, wide).transpose(2, 1, 0, 3, 4)
        grad = grad.reshape(Y, Z, deep, wide)
        half = pick(grad, y, 0) + partner(pick(grad, 1 - y, 0).astype(BF), "y").astype(F32)
        total = pick(half, z, 0)
        for s in range(1, Z):
            total = total + partner(pick(half, z ^ s, 0).astype(BF), "z", s).astype(F32)
        if blocks > 1:
            total = lax.psum_scatter(total, "blk", scatter_dimension=0, tiled=True)
        return total

    output_owned = data_scatter(output_grad).T
    qkv_owned = data_scatter(qkv_grad)
    query_owned = qkv_owned[:, :query_wide]
    pair_owned = jnp.stack([qkv_owned[:, query_wide:first_pair], qkv_owned[:, first_pair:]])
    gain_two, router_grad = lax.psum((gain_part_two, router_part), EVERY)
    for axis, mask in (("core", 1), ("x", 1), ("y", 1), ("z", 1), ("z", 2)):
        gain_one = gain_one + partner(gain_one, axis, mask)
    if blocks > 1:
        gain_one = lax.psum(gain_one, "blk")
    gain_grad = jnp.stack([gain_one, gain_two])
    rate_wide = 2.0 * D ** (-0.5)
    rate_output = 2.0 * max(1, 2 * H * HD // group_rows) ** (-0.5)
    rate_router = 2.0 * (4 * D) ** (-0.5)
    rate_down = 2.0 * (FF // 16) ** (-0.5)
    query_new = adam_update(
        query_weight, query_owned, query_moment, query_second, rate_wide, WEIGHT_DECAY
    )
    pair_new = adam_update(
        key_value_weight, pair_owned, key_value_moment, key_value_second, rate_wide, WEIGHT_DECAY
    )
    output_new = adam_update(
        output_weight, output_owned, output_moment, output_second, rate_output, WEIGHT_DECAY
    )
    router_new = adam_update(
        router_weight, router_grad, router_moment, router_second, rate_router, WEIGHT_DECAY
    )
    gate_up_new = adam_update(
        gate_up_weight, gate_up_grad, gate_up_moment, gate_up_second, rate_wide, WEIGHT_DECAY
    )
    down_new = adam_update(
        down_weight, down_owned, down_moment, down_second, rate_down, WEIGHT_DECAY
    )
    gains_new = adam_update(norm_gains, gain_grad, gains_moment, gains_second, 0.2, 0.0)
    return (
        (result, stream_grad)
        + query_new
        + pair_new
        + output_new
        + router_new
        + gate_up_new
        + down_new
        + gains_new
    )


def solution(mesh):
    data_size, tensor_size = mesh.shape["dp"], mesh.shape["tensor"]
    blocks = data_size // (Z * Y)
    fine = Mesh(mesh.devices.reshape(blocks, Z, Y, tensor_size // C, C), EVERY)
    split = ("x", "core")
    rows = P(EVERY, None)
    wide = P(DATA, split)
    pair = P(None, DATA, split)
    tall = P(split, DATA)
    gate_up = P(None, None, DATA, split)
    down = P(None, split, DATA)
    group = P(DATA, None)
    return jax.shard_map(
        body,
        mesh=fine,
        in_specs=(rows, rows, group, group)
        + (wide,) * 3
        + (pair,) * 3
        + (tall,) * 3
        + (P(),) * 3
        + (gate_up,) * 3
        + (down,) * 3
        + (P(),) * 3,
        out_specs=(rows, rows)
        + (wide,) * 3
        + (pair,) * 3
        + (tall,) * 3
        + (P(),) * 3
        + (gate_up,) * 3
        + (down,) * 3
        + (P(),) * 3,
        check_vma=False,
    )
```

time: 2890 us -> 1180 us (0.41)
  waiting for transfers between devices: 1570 us -> 352 us
  other arithmetic: 454 us -> 154 us
  matrix products: 370 us -> 84.2 us
  starting transfers between devices: 0.91 us -> 94.5 us
  Pallas kernels: 0 us -> 78.2 us
  local copies, waits for them, and re-layouts: 324 us -> 275 us
    reduce_scatter x11 -> x0, waiting for transfers between devices: 1180 us -> none  [the longest x1 285 us: body(): lax.psum_scatter(up_whole, 'dp', scatter_dimension=1, tiled=True)]
    scatter-add x16 -> x0, other arithmetic: 370 us -> none  [the longest x8 185 us: expert_work(): row_grads.at[slots_here].add(slot_back.reshape(together * capacity, D))]
    ppermute x0 -> x73, waiting for transfers between devices: none -> 351 us  [partner(): return lax.ppermute(value, axis, [(i, i ^ mask) for i in range(size)])]
    all_gather x6 -> x0, waiting for transfers between devices: 336 us -> none  [the longest x1 229 us: body(): lax.all_gather(gate_up_weight.astype(jnp.bfloat16), 'dp', axis=2, tiled=T...]
    dot_general x87 -> x15, matrix products: 339 us -> 68.3 us  [the longest x1 23.6 us: body(): lax.dot_general(rows_all, jnp.concatenate(hidden_parts, 0), (((0,), (0,))...]
    gather x17 -> x0, local copies, waits for them, and re-layouts: 225 us -> none  [the longest x8 102 us: expert_work(): inputs_here = padded_rows[slots_here].reshape(together, capacity, D)]
    ppermute x0 -> x73, starting transfers between devices: none -> 94.5 us  [partner(): return lax.ppermute(value, axis, [(i, i ^ mask) for i in range(size)])]
    all_gather x3 -> x0, blocking collectives: 87.9 us -> none  [the longest x1 33.2 us: body(): lax.all_gather(query_weight.astype(jnp.bfloat16), 'dp', axis=0, tiled=True)]
  transfers between devices with their start and end apart: 18 -> 74, of which waited for: 15 -> 23; matrix products, arithmetic and copies ran while one was open for 7% -> 27% of each run, Pallas kernels for 0% -> 5%
where the time goes in v1:
time: 1180 us; the launch traced here: 1160 us
  waiting for transfers between devices  352 us (30%)
  local copies, waits for them, and re-layouts  275 us (23%)
  other arithmetic  154 us (13%)
  blocking collectives  110 us (9%)
  starting transfers between devices  94.5 us (8%)
  matrix products  84.2 us (7%)
  Pallas kernels  78.2 us (7%)
  between operations  17.2 us (1%)
    ppermute x73, waiting for transfers between devices, partner(): return lax.ppermute(value, axis, [(i, i ^ mask) for i in range(size)])  351 us
    psum x1, blocking collectives, body(): gain_two, router_grad = lax.psum((gain_part_two, router_part), EVERY)  110 us
    ppermute x73, starting transfers between devices, partner(): return lax.ppermute(value, axis, [(i, i ^ mask) for i in range(size)])  94.5 us
    pallas_call x4, Pallas kernels, expert_chunk(): pl.pallas_call(expert_kernel, grid_spec=pltpu.PrefetchScalarGridSpec(num_...  78.2 us
    unnamed x327, local copies, waits for them, and re-layouts  71.8 us
    reshape x2, local copies, waits for them, and re-layouts, body(): hidden_grad.reshape(blocks, Z, Y, depth, together, 2, X, C, lane_wide)  35.4 us
    transpose x1, local copies, waits for them, and re-layouts, body(): grid.transpose(4, 5, 2, 0, 6, 7, 1, 3, 8).reshape(together, D, 3 * FF)  31.3 us
    slice x8, local copies, waits for them, and re-layouts, to_absolute(): parts = [lax.slice_in_dim(stacked, k, k + 1, axis=dim) for k in order]  29.1 us
  transfers between devices with their start and end apart: 74, of which 23 were waited for; matrix products, arithmetic and copies ran while one was open for 27% of the time, Pallas kernels for 5%

profile of v1, /device:TPU:0, one launch (start us, length us, event | category | flops | bytes accessed | tf_op | source)
XLA Modules:
  0.0 1164.7 jit_solution(426173101361360468)
XLA Ops:
  42.5 13.2 %collective-permute-done.6 = bf16[4,128,768]{2,1,0:T(8,128)(2,1)S(1)} collective-permute-done((bf16[4,128,768]{2,1,0:T(8,128)(2,1)S(1)}, bf16[4,128,768]{2,1,0:T(8,128)(2,1)S(1)}, u32[]{:S(2)}, u32[]{:S(2)}) %collective-permute-start.6) | collective-permute-done | bytes 786464 | tf_op jit(solution)/shard_map/ppermute | solution.py:72
  90.6 19.6 %collective-permute-done.24.b0 = bf16[256,1024]{1,0:T(8,128)(2,1)S(1)} collective-permute-done((bf16[256,1024]{1,0:T(8,128)(2,1)}, bf16[256,1024]{1,0:T(8,128)(2,1)S(1)}, u32[]{:S(2)}, u32[]{:S(2)}) %collective-permute-start.24) | collective-permute-done | bytes 524320 | tf_op jit(solution)/shard_map/ppermute | solution.py:72
  115.9 73.4 %collective-permute-done.30.b0 = bf16[256,1024]{1,0:T(8,128)(2,1)S(1)} collective-permute-done((bf16[256,1024]{1,0:T(8,128)(2,1)}, bf16[256,1024]{1,0:T(8,128)(2,1)S(1)}, u32[]{:S(2)}, u32[]{:S(2)}) %collective-permute-start.30) | collective-permute-done | bytes 524320 | tf_op jit(solution)/shard_map/ppermute | solution.py:72
  266.4 8.0 collective-permute-done.15
  286.4 11.8 %collective-permute-done.16 = bf16[4,4,128,384]{3,2,1,0:T(8,128)(2,1)} collective-permute-done((bf16[4,4,128,384]{3,2,1,0:T(8,128)(2,1)}, bf16[4,4,128,384]{3,2,1,0:T(8,128)(2,1)}, u32[]{:S(2)}, u32[]{:S(2)}) %collective-permute-start.16) | collective-permute-done | bytes 1572896 | tf_op jit(solution)/shard_map/ppermute | solution.py:72
  300.8 7.3 collective-permute-done.18
  314.8 25.5 %collective-permute-done.20 = bf16[4,4,128,384]{3,2,1,0:T(8,128)(2,1)} collective-permute-done((bf16[4,4,128,384]{3,2,1,0:T(8,128)(2,1)}, bf16[4,4,128,384]{3,2,1,0:T(8,128)(2,1)}, u32[]{:S(2)}, u32[]{:S(2)}) %collective-permute-start.20) | collective-permute-done | bytes 1572896 | tf_op jit(solution)/shard_map/ppermute | solution.py:72
  352.3 8.6 copy.193
  360.9 8.7 copy.194
  374.8 12.3 %maximum_select_fusion = bf16[2,2,4,2,4,1,128,3,128]{6,8,7,4,3,2,1,5,0:T(8,128)(2,1)S(1)} fusion(bf16[1,2,4,2,4,1,128,3,128]{6,8,7,4,3,2,1,5,0:T(8,128)(2,1)} %bitcast.399, bf16[1,2,4,2,4,1,128,3,128]{6,8,7,4,3,2,1,5,0:T(8,128)(2,1)} %bitcast.394, bf16[1,1,4,1,4,1,128,3,128]{6,8,7,4,3,2,1,5,0:T(8,128)(2,1)} %bitcast.439, ...), kind=kLoop, calls=%fused_computation.10 | loop fusion | flops 56623104 | bytes 37748736 | tf_op jit(solution)/shard_map/jit(_where)/select_n | solution.py:82
  392.3 9.4 maximum_select_fusion.1
  407.7 16.2 %fusion.8 = bf16[4,1,4,2,128,3,2,2,128]{4,8,5,0,7,2,6,1,3:T(8,128)(2,1)} fusion(bf16[2,2,2,2,4,1,128,3,128]{6,8,7,4,3,2,1,5,0:T(8,128)(2,1)} %get-tuple-element.184, bf16[2,2,2,2,4,1,128,3,128]{6,8,7,4,3,2,1,5,0:T(8,128)(2,1)} %get-tuple-element.183, pred[]{:T(512)S(6)} %ne.8, bf16[2,2,1,2,4,1,128,3,128]{6,8,7,4,3,2,1,5,0:T(8,128)(2,1)S(1)} %copy-done.27, ...), kind=kLoop, calls=%fused_computation.13 | loop fusion | flops 94371840 | bytes 62914564 | tf_op jit(solution)/shard_map/transpose | solution.py:307
  423.9 31.3 %copy.211 = bf16[4,1,4,2,128,3,2,2,128]{8,7,6,5,4,3,2,0,1:T(2,128)(2,1)} copy(bf16[4,1,4,2,128,3,2,2,128]{4,8,5,0,7,2,6,1,3:T(8,128)(2,1)} %fusion.8) | data formatting | bytes 25165824 | tf_op jit(solution)/shard_map/transpose | solution.py:307
  455.2 27.3 %reshape.674.w = bf16[4,1024,1536]{2,1,0:T(8,128)(2,1)} reshape(bf16[4,1,4,2,128,3,2,2,128]{8,7,6,5,4,3,2,0,1:T(2,128)(2,1)} %copy.211) | data formatting | bytes 25165824 | tf_op jit(solution)/shard_map/reshape | solution.py:307
  482.6 19.7 %experts.5 = (bf16[512,4096]{1,0:T(8,128)(2,1)}, bf16[512,2048]{1,0:T(8,128)(2,1)}, bf16[512,1024]{1,0:T(8,128)(2,1)S(1)}, bf16[512,1152]{1,0:T(8,128)(2,1)S(1)}) custom-call(s32[1]{0:T(128)} %bitcast.37.base, bf16[256,1152]{1,0:T(8,128)(2,1)} %collective-permute-done.22.r0, bf16[256,1152]{1,0:T(8,128)(2,1)} %collective-permute-done.23.r1, ...), custom_call_target="tpu_custom_call" | custom-call | flops 12884901888 | bytes 20971520 | tf_op jit(solution)/shard_map/experts/pallas_call | solution.py:162
  503.5 19.5 %experts.6 = (bf16[512,4096]{1,0:T(8,128)(2,1)}, bf16[512,2048]{1,0:T(8,128)(2,1)}, bf16[512,1024]{1,0:T(8,128)(2,1)S(1)}, bf16[512,1152]{1,0:T(8,128)(2,1)S(1)}) custom-call(s32[1]{0:T(128)} %bitcast.37.base, bf16[256,1152]{1,0:T(8,128)(2,1)} %collective-permute-done.28.r0, bf16[256,1152]{1,0:T(8,128)(2,1)S(1)} %collective-permute-done.29.r1, ...), custom_call_target="tpu_custom_call" | custom-call | flops 12884901888 | bytes 20971520 | tf_op jit(solution)/shard_map/experts/pallas_call | solution.py:162
  524.6 19.2 %experts.7 = (bf16[512,4096]{1,0:T(8,128)(2,1)}, bf16[512,2048]{1,0:T(8,128)(2,1)}, bf16[512,1024]{1,0:T(8,128)(2,1)S(1)}, bf16[512,1152]{1,0:T(8,128)(2,1)S(1)}) custom-call(s32[1]{0:T(128)} %bitcast.37.base, bf16[256,1152]{1,0:T(8,128)(2,1)} %collective-permute-done.34.r0, bf16[256,1152]{1,0:T(8,128)(2,1)S(1)} %copy-done.23, ...), custom_call_target="tpu_custom_call" | custom-call | flops 12884901888 | bytes 20971520 | tf_op jit(solution)/shard_map/experts/pallas_call | solution.py:162
  547.1 19.7 %experts.4 = (bf16[512,4096]{1,0:T(8,128)(2,1)}, bf16[512,2048]{1,0:T(8,128)(2,1)}, bf16[512,1024]{1,0:T(8,128)(2,1)S(1)}, bf16[512,1152]{1,0:T(8,128)(2,1)S(1)}) custom-call(s32[1]{0:T(128)} %bitcast.37.base, bf16[256,1152]{1,0:T(8,128)(2,1)S(1)} %copy-done.13, bf16[256,1152]{1,0:T(8,128)(2,1)S(1)} %copy-done.21, bf16[256,1024]{1,0:T(8,128)(2,1)} %get-tuple-element.163.b0, ...), custom_call_target="tpu_custom_call" | custom-call | flops 12884901888 | bytes 20971520 | tf_op jit(solution)/shard_map/experts/pallas_call | solution.py:162
  566.8 23.6 %fusion.23 = bf16[1024,4096]{1,0:T(8,128)(2,1)} fusion(bf16[2048,1024]{1,0:T(8,128)(2,1)S(1)} %copy-done.111, bf16[512,4096]{1,0:T(8,128)(2,1)} %get-tuple-element.50, bf16[512,4096]{1,0:T(8,128)(2,1)} %get-tuple-element.49, bf16[512,4096]{1,0:T(8,128)(2,1)} %get-tuple-element.48, bf16[512,4096]{1,0:T(8,128)(2,1)} %get-tuple-element.47), kind=kOutput, calls=%fused_computation.39 | convolution fusion | flops 17251172352 | bytes 29360128 | tf_op jit(solution)/shard_map/dot_general | solution.py:398
  590.4 13.2 %fusion.32 = bf16[1024,2048]{1,0:T(8,128)(2,1)} fusion(bf16[2048,1024]{1,0:T(8,128)(2,1)S(1)} %copy-done.110, bf16[512,2048]{1,0:T(8,128)(2,1)} %get-tuple-element.54, bf16[512,2048]{1,0:T(8,128)(2,1)} %get-tuple-element.53, bf16[512,2048]{1,0:T(8,128)(2,1)S(1)} %copy-done.136, bf16[512,2048]{1,0:T(8,128)(2,1)} %get-tuple-element.51), kind=kOutput, calls=%fused_computation.71 | convolution fusion | flops 8625586176 | bytes 16777216 | tf_op jit(solution)/shard_map/dot_general | solution.py:404
  606.1 14.3 %reshape.681 = bf16[1,4,2,128,4,2,2,2,128]{8,7,6,5,4,3,2,1,0:T(2,128)(2,1)} reshape(bf16[1024,4096]{1,0:T(8,128)(2,1)} %fusion.23) | data formatting | bytes 16777216 | tf_op jit(solution)/shard_map/reshape | solution.py:413
  620.4 21.2 %copy.227 = bf16[1,4,2,128,4,2,2,2,128]{3,8,5,4,1,2,6,0,7:T(8,128)(2,1)} copy(bf16[1,4,2,128,4,2,2,2,128]{8,7,6,5,4,3,2,1,0:T(2,128)(2,1)} %reshape.681) | data formatting | bytes 16777216 | tf_op jit(solution)/shard_map/reshape | solution.py:413
  641.5 7.7 reshape.682
  649.2 11.2 copy.228
  673.3 16.9 %collective-permute-done.42 = bf16[256,1152]{1,0:T(8,128)(2,1)S(1)} collective-permute-done((bf16[256,1152]{1,0:T(8,128)(2,1)S(1)}, bf16[256,1152]{1,0:T(8,128)(2,1)S(1)}, u32[]{:S(2)}, u32[]{:S(2)}) %collective-permute-start.42) | collective-permute-done | bytes 589856 | tf_op jit(solution)/shard_map/ppermute | solution.py:72
  692.0 16.1 %collective-permute-done.44 = bf16[256,1152]{1,0:T(8,128)(2,1)S(1)} collective-permute-done((bf16[256,1152]{1,0:T(8,128)(2,1)S(1)}, bf16[256,1152]{1,0:T(8,128)(2,1)S(1)}, u32[]{:S(2)}, u32[]{:S(2)}) %collective-permute-start.44) | collective-permute-done | bytes 589856 | tf_op jit(solution)/shard_map/ppermute | solution.py:72
  715.9 38.6 %collective-permute-done.33 = bf16[256,1024]{1,0:T(8,128)(2,1)S(1)} collective-permute-done((bf16[256,1024]{1,0:T(8,128)(2,1)S(1)}, bf16[256,1024]{1,0:T(8,128)(2,1)S(1)}, u32[]{:S(2)}, u32[]{:S(2)}) %collective-permute-start.33) | collective-permute-done | bytes 524320 | tf_op jit(solution)/shard_map/ppermute | solution.py:72
  782.0 110.0 %psum.15 = f32[1,1024]{1,0:T(1,128)S(1)} all-reduce(f32[1,1024]{1,0:T(1,128)S(1)} %bitcast.495), channel_id=1, replica_groups=mesh['blk'=1,'z'=4,'y'=2,'x'=2,'core'=2] {'blk','z','y','x','core'}, use_global_device_ids=true, to_apply=%region_20.21 | all-reduce | flops 1024 | bytes 8192 | tf_op jit(solution)/shard_map/psum | solution.py:516
  955.2 40.7 %collective-permute-done.52 = bf16[4,128,512]{2,1,0:T(8,128)(2,1)S(1)} collective-permute-done((bf16[4,128,512]{2,1,0:T(8,128)(2,1)S(1)}, bf16[4,128,512]{2,1,0:T(8,128)(2,1)S(1)}, u32[]{:S(2)}, u32[]{:S(2)}) %collective-permute-start.52) | collective-permute-done | bytes 524320 | tf_op jit(solution)/shard_map/ppermute | solution.py:72
  1025.6 38.1 %collective-permute-done.55 = bf16[128,512]{1,0:T(8,128)(2,1)} collective-permute-done((bf16[128,512]{1,0:T(8,128)(2,1)}, bf16[128,512]{1,0:T(8,128)(2,1)}, u32[]{:S(2)}, u32[]{:S(2)}) %collective-permute-start.55) | collective-permute-done | bytes 131104 | tf_op jit(solution)/shard_map/ppermute | solution.py:72
  1069.3 8.1 collective-permute-done.51
  1087.6 23.0 %collective-permute-start.71 = (f32[1024]{0:T(1024)S(1)}, f32[1024]{0:T(1024)S(1)}, u32[]{:S(2)}, u32[]{:S(2)}) collective-permute-start(f32[1024]{0:T(1024)S(1)} %add.485), channel_id=1, source_target_pairs={{0,8},{8,0},{16,24},{24,16},{1,9},{9,1},{17,25},{25,17},{2,10},{10... | collective-permute-start | bytes 12296 | tf_op jit(solution)/shard_map/ppermute | solution.py:72
  (649 shorter events, 414.1 us)
Async XLA Ops:
  7.2 1008.2 %all-reduce.2.cloned.1.call-start = ((), (), s32[]{:S(2)}) async-start(), calls=%async_computation | async-start | bytes 262144 | tf_op jit(solution)/shard_map/psum | solution.py:516
  82.1 107.8 %collective-permute-start.12 = (bf16[2,4,128,384]{3,2,1,0:T(8,128)(2,1)}, bf16[2,4,128,384]{3,2,1,0:T(8,128)(2,1)}, u32[]{:S(2)}, u32[]{:S(2)}) collective-permute-start(bf16[2,4,128,384]{3,2,1,0:T(8,128)(2,1)} %get-tuple-element.210), channel_id=1, source_target_pairs={{0,8},{8,0},{16,24},{24,16},{1,9},{9,1},{17,25},{25,17},{2,10},{10... | collective-permute-start | bytes 2359304 | tf_op jit(solution)/shard_map/ppermute | solution.py:72
  83.5 106.9 %collective-permute-start.13 = (bf16[2,4,128,384]{3,2,1,0:T(8,128)(2,1)}, bf16[2,4,128,384]{3,2,1,0:T(8,128)(2,1)}, u32[]{:S(2)}, u32[]{:S(2)}) collective-permute-start(bf16[2,4,128,384]{3,2,1,0:T(8,128)(2,1)} %get-tuple-element.211), channel_id=1, source_target_pairs={{0,16},{8,24},{16,0},{24,8},{1,17},{9,25},{17,1},{25,9},{2,18},{10... | collective-permute-start | bytes 2359304 | tf_op jit(solution)/shard_map/ppermute | solution.py:72
  85.6 104.9 %collective-permute-start.14 = (bf16[2,4,128,384]{3,2,1,0:T(8,128)(2,1)}, bf16[2,4,128,384]{3,2,1,0:T(8,128)(2,1)}, u32[]{:S(2)}, u32[]{:S(2)}) collective-permute-start(bf16[2,4,128,384]{3,2,1,0:T(8,128)(2,1)} %get-tuple-element.212), channel_id=1, source_target_pairs={{0,24},{8,16},{16,8},{24,0},{1,25},{9,17},{17,9},{25,1},{2,26},{10... | collective-permute-start | bytes 2359304 | tf_op jit(solution)/shard_map/ppermute | solution.py:72
  87.1 102.2 %collective-permute-start.30 = (bf16[256,1024]{1,0:T(8,128)(2,1)}, bf16[256,1024]{1,0:T(8,128)(2,1)S(1)}, u32[]{:S(2)}, u32[]{:S(2)}) collective-permute-start(bf16[256,1024]{1,0:T(8,128)(2,1)} %get-tuple-element.163.b0), channel_id=1, source_target_pairs={{0,16},{8,24},{16,0},{24,8},{1,17},{9,25},{17,1},{25,9},{2,18},{10... | collective-permute-start | bytes 1572872 | tf_op jit(solution)/shard_map/ppermute | solution.py:72
  110.2 79.6 %collective-permute-start.36 = (bf16[256,1024]{1,0:T(8,128)(2,1)}, bf16[256,1024]{1,0:T(8,128)(2,1)S(1)}, u32[]{:S(2)}, u32[]{:S(2)}) collective-permute-start(bf16[256,1024]{1,0:T(8,128)(2,1)} %get-tuple-element.163.b0), channel_id=1, source_target_pairs={{0,24},{8,16},{16,8},{24,0},{1,25},{9,17},{17,9},{25,1},{2,26},{10... | collective-permute-start | bytes 1572872 | tf_op jit(solution)/shard_map/ppermute | solution.py:72
  190.4 46.4 %collective-permute-start.31 = (bf16[256,1024]{1,0:T(8,128)(2,1)S(1)}, bf16[256,1024]{1,0:T(8,128)(2,1)}, u32[]{:S(2)}, u32[]{:S(2)}) collective-permute-start(bf16[256,1024]{1,0:T(8,128)(2,1)S(1)} %collective-permute-done.30.b0), channel_id=1, source_target_pairs={{0,1},{1,0},{2,3},{3,2},{4,5},{5,4},{6,7},{7,6},{8,9},{9,8},{10,11... | collective-permute-start | bytes 1572872 | tf_op jit(solution)/shard_map/ppermute | solution.py:72
  190.5 52.1 %collective-permute-start.37 = (bf16[256,1024]{1,0:T(8,128)(2,1)S(1)}, bf16[256,1024]{1,0:T(8,128)(2,1)S(1)}, u32[]{:S(2)}, u32[]{:S(2)}) collective-permute-start(bf16[256,1024]{1,0:T(8,128)(2,1)S(1)} %collective-permute-done.36.b0), channel_id=1, source_target_pairs={{0,1},{1,0},{2,3},{3,2},{4,5},{5,4},{6,7},{7,6},{8,9},{9,8},{10,11... | collective-permute-start | bytes 1572872 | tf_op jit(solution)/shard_map/ppermute | solution.py:72
  216.6 47.1 %collective-permute-start.19 = (bf16[4,4,128,384]{3,2,1,0:T(8,128)(2,1)}, bf16[4,4,128,384]{3,2,1,0:T(8,128)(2,1)}, u32[]{:S(2)}, u32[]{:S(2)}) collective-permute-start(bf16[4,4,128,384]{3,2,1,0:T(8,128)(2,1)} %get-tuple-element.207), channel_id=1, source_target_pairs={{0,4},{4,0},{1,5},{5,1},{2,6},{6,2},{3,7},{7,3},{8,12},{12,8},{9,1... | collective-permute-start | bytes 4718600 | tf_op jit(solution)/shard_map/ppermute | solution.py:72
  259.0 49.1 %collective-permute-start.18 = (bf16[4,4,128,384]{3,2,1,0:T(8,128)(2,1)}, bf16[4,4,128,384]{3,2,1,0:T(8,128)(2,1)}, u32[]{:S(2)}, u32[]{:S(2)}) collective-permute-start(bf16[4,4,128,384]{3,2,1,0:T(8,128)(2,1)} %get-tuple-element.207), channel_id=1, source_target_pairs={{0,2},{2,0},{1,3},{3,1},{4,6},{6,4},{5,7},{7,5},{8,10},{10,8},{9,1... | collective-permute-start | bytes 4718600 | tf_op jit(solution)/shard_map/ppermute | solution.py:72
  263.8 76.5 %collective-permute-start.20 = (bf16[4,4,128,384]{3,2,1,0:T(8,128)(2,1)}, bf16[4,4,128,384]{3,2,1,0:T(8,128)(2,1)}, u32[]{:S(2)}, u32[]{:S(2)}) collective-permute-start(bf16[4,4,128,384]{3,2,1,0:T(8,128)(2,1)} %collective-permute-done.19), channel_id=1, source_target_pairs={{0,2},{2,0},{1,3},{3,1},{4,6},{6,4},{5,7},{7,5},{8,10},{10,8},{9,1... | collective-permute-start | bytes 4718600 | tf_op jit(solution)/shard_map/ppermute | solution.py:72
  274.4 68.1 %collective-permute-start.17 = (bf16[4,4,128,384]{3,2,1,0:T(8,128)(2,1)}, bf16[4,4,128,384]{3,2,1,0:T(8,128)(2,1)}, u32[]{:S(2)}, u32[]{:S(2)}) collective-permute-start(bf16[4,4,128,384]{3,2,1,0:T(8,128)(2,1)} %collective-permute-done.15), channel_id=1, source_target_pairs={{0,4},{4,0},{1,5},{5,1},{2,6},{6,2},{3,7},{7,3},{8,12},{12,8},{9,1... | collective-permute-start | bytes 4718600 | tf_op jit(solution)/shard_map/ppermute | solution.py:72
  503.5 162.1 %collective-permute-start.26 = (bf16[256,1024]{1,0:T(8,128)(2,1)}, bf16[256,1024]{1,0:T(8,128)(2,1)}, u32[]{:S(2)}, u32[]{:S(2)}) collective-permute-start(bf16[256,1024]{1,0:T(8,128)(2,1)} %slice.390), channel_id=1, source_target_pairs={{0,1},{1,0},{2,3},{3,2},{4,5},{5,4},{6,7},{7,6},{8,9},{9,8},{10,11... | collective-permute-start | bytes 1572872 | tf_op jit(solution)/shard_map/ppermute | solution.py:72
  524.2 141.9 %collective-permute-start.32 = (bf16[256,1024]{1,0:T(8,128)(2,1)}, bf16[256,1024]{1,0:T(8,128)(2,1)}, u32[]{:S(2)}, u32[]{:S(2)}) collective-permute-start(bf16[256,1024]{1,0:T(8,128)(2,1)} %slice.392), channel_id=1, source_target_pairs={{0,1},{1,0},{2,3},{3,2},{4,5},{5,4},{6,7},{7,6},{8,9},{9,8},{10,11... | collective-permute-start | bytes 1572872 | tf_op jit(solution)/shard_map/ppermute | solution.py:72
  544.7 126.3 %collective-permute-start.38 = (bf16[256,1024]{1,0:T(8,128)(2,1)}, bf16[256,1024]{1,0:T(8,128)(2,1)}, u32[]{:S(2)}, u32[]{:S(2)}) collective-permute-start(bf16[256,1024]{1,0:T(8,128)(2,1)} %slice.394), channel_id=1, source_target_pairs={{0,1},{1,0},{2,3},{3,2},{4,5},{5,4},{6,7},{7,6},{8,9},{9,8},{10,11... | collective-permute-start | bytes 1572872 | tf_op jit(solution)/shard_map/ppermute | solution.py:72
  545.7 114.7 %collective-permute-start.41 = (bf16[256,1152]{1,0:T(8,128)(2,1)}, bf16[256,1152]{1,0:T(8,128)(2,1)}, u32[]{:S(2)}, u32[]{:S(2)}) collective-permute-start(bf16[256,1152]{1,0:T(8,128)(2,1)} %slice.398), channel_id=1, source_target_pairs={{0,1},{1,0},{2,3},{3,2},{4,5},{5,4},{6,7},{7,6},{8,9},{9,8},{10,11... | collective-permute-start | bytes 1769480 | tf_op jit(solution)/shard_map/ppermute | solution.py:72
  546.9 115.3 %collective-permute-start.43 = (bf16[256,1152]{1,0:T(8,128)(2,1)}, bf16[256,1152]{1,0:T(8,128)(2,1)}, u32[]{:S(2)}, u32[]{:S(2)}) collective-permute-start(bf16[256,1152]{1,0:T(8,128)(2,1)} %slice.400), channel_id=1, source_target_pairs={{0,1},{1,0},{2,3},{3,2},{4,5},{5,4},{6,7},{7,6},{8,9},{9,8},{10,11... | collective-permute-start | bytes 1769480 | tf_op jit(solution)/shard_map/ppermute | solution.py:72
  690.3 64.2 %collective-permute-start.33 = (bf16[256,1024]{1,0:T(8,128)(2,1)S(1)}, bf16[256,1024]{1,0:T(8,128)(2,1)S(1)}, u32[]{:S(2)}, u32[]{:S(2)}) collective-permute-start(bf16[256,1024]{1,0:T(8,128)(2,1)S(1)} %add_convert_fusion.4), channel_id=1, source_target_pairs={{0,16},{8,24},{16,0},{24,8},{1,17},{9,25},{17,1},{25,9},{2,18},{10... | collective-permute-start | bytes 1572872 | tf_op jit(solution)/shard_map/ppermute | solution.py:72
  708.1 46.3 %collective-permute-start.39 = (bf16[256,1024]{1,0:T(8,128)(2,1)S(1)}, bf16[256,1024]{1,0:T(8,128)(2,1)S(1)}, u32[]{:S(2)}, u32[]{:S(2)}) collective-permute-start(bf16[256,1024]{1,0:T(8,128)(2,1)S(1)} %add_convert_fusion.3), channel_id=1, source_target_pairs={{0,24},{8,16},{16,8},{24,0},{1,25},{9,17},{17,9},{25,1},{2,26},{10... | collective-permute-start | bytes 1572872 | tf_op jit(solution)/shard_map/ppermute | solution.py:72
  762.2 129.8 %collective-permute-start.47 = (bf16[256,1024]{1,0:T(8,128)(2,1)}, bf16[256,1024]{1,0:T(8,128)(2,1)}, u32[]{:S(2)}, u32[]{:S(2)}) collective-permute-start(bf16[256,1024]{1,0:T(8,128)(2,1)} %get-tuple-element.177), channel_id=1, source_target_pairs={{0,1},{1,0},{2,3},{3,2},{4,5},{5,4},{6,7},{7,6},{8,9},{9,8},{10,11... | collective-permute-start | bytes 1572872 | tf_op jit(solution)/shard_map/ppermute | solution.py:72
  769.0 123.0 %collective-permute-start.49 = (bf16[256,1024]{1,0:T(8,128)(2,1)}, bf16[256,1024]{1,0:T(8,128)(2,1)}, u32[]{:S(2)}, u32[]{:S(2)}) collective-permute-start(bf16[256,1024]{1,0:T(8,128)(2,1)} %collective-permute-done.48), channel_id=1, source_target_pairs={{0,1},{1,0},{2,3},{3,2},{4,5},{5,4},{6,7},{7,6},{8,9},{9,8},{10,11... | collective-permute-start | bytes 1572872 | tf_op jit(solution)/shard_map/ppermute | solution.py:72
  775.8 170.5 %collective-permute-start.62 = (bf16[2,4,4,128,384]{3,4,2,1,0:T(8,128)(2,1)}, bf16[2,4,4,128,384]{3,4,2,1,0:T(8,128)(2,1)}, u32[]{:S(2)}, u32[]{:S(2)}) collective-permute-start(bf16[2,4,4,128,384]{3,4,2,1,0:T(8,128)(2,1)} %bitcast.458), channel_id=1, source_target_pairs={{0,2},{2,0},{1,3},{3,1},{4,6},{6,4},{5,7},{7,5},{8,10},{10,8},{9,1... | collective-permute-start | bytes 9437192 | tf_op jit(solution)/shard_map/ppermute | solution.py:72
  779.4 162.2 %collective-permute-start.60 = (bf16[2,4,4,128,384]{3,4,2,1,0:T(8,128)(2,1)}, bf16[2,4,4,128,384]{3,4,2,1,0:T(8,128)(2,1)}, u32[]{:S(2)}, u32[]{:S(2)}) collective-permute-start(bf16[2,4,4,128,384]{3,4,2,1,0:T(8,128)(2,1)} %dynamic-slice_bitcast_fusion), channel_id=1, source_target_pairs={{0,4},{4,0},{1,5},{5,1},{2,6},{6,2},{3,7},{7,3},{8,12},{12,8},{9,1... | collective-permute-start | bytes 9437192 | tf_op jit(solution)/shard_map/ppermute | solution.py:72
  944.8 55.1 %collective-permute-start.61 = (bf16[4,4,128,384]{2,3,1,0:T(8,128)(2,1)S(1)}, bf16[4,4,128,384]{2,3,1,0:T(8,128)(2,1)S(1)}, u32[]{:S(2)}, u32[]{:S(2)}) collective-permute-start(bf16[4,4,128,384]{2,3,1,0:T(8,128)(2,1)S(1)} %fusion.43), channel_id=1, source_target_pairs={{0,2},{2,0},{1,3},{3,1},{4,6},{6,4},{5,7},{7,5},{8,10},{10,8},{9,1... | collective-permute-start | bytes 4718600 | tf_op jit(solution)/shard_map/ppermute | solution.py:72
  949.6 52.2 %collective-permute-start.63 = (bf16[4,4,128,384]{2,3,1,0:T(8,128)(2,1)S(1)}, bf16[4,4,128,384]{2,3,1,0:T(8,128)(2,1)S(1)}, u32[]{:S(2)}, u32[]{:S(2)}) collective-permute-start(bf16[4,4,128,384]{2,3,1,0:T(8,128)(2,1)S(1)} %fusion.40), channel_id=1, source_target_pairs={{0,4},{4,0},{1,5},{5,1},{2,6},{6,2},{3,7},{7,3},{8,12},{12,8},{9,1... | collective-permute-start | bytes 4718600 | tf_op jit(solution)/shard_map/ppermute | solution.py:72
  953.0 111.8 %collective-permute-start.50 = (bf16[2,256,1024]{2,1,0:T(8,128)(2,1)}, bf16[2,256,1024]{2,1,0:T(8,128)(2,1)S(1)}, u32[]{:S(2)}, u32[]{:S(2)}) collective-permute-start(bf16[2,256,1024]{2,1,0:T(8,128)(2,1)} %pad_maximum_fusion.10), channel_id=1, source_target_pairs={{0,1},{1,0},{2,3},{3,2},{4,5},{5,4},{6,7},{7,6},{8,9},{9,8},{10,11... | collective-permute-start | bytes 3145736 | tf_op jit(solution)/shard_map/ppermute | solution.py:72
  953.1 51.1 %collective-permute-start.57 = (bf16[128,256]{1,0:T(8,128)(2,1)S(1)}, bf16[128,256]{1,0:T(8,128)(2,1)S(1)}, u32[]{:S(2)}, u32[]{:S(2)}) collective-permute-start(bf16[128,256]{1,0:T(8,128)(2,1)S(1)} %get-tuple-element.239), channel_id=1, source_target_pairs={{0,8},{8,0},{16,24},{24,16},{1,9},{9,1},{17,25},{25,17},{2,10},{10... | collective-permute-start | bytes 196616 | tf_op jit(solution)/shard_map/ppermute | solution.py:72
  1006.9 60.1 %collective-permute-start.64 = (bf16[2,4,128,384]{2,3,1,0:T(8,128)(2,1)}, bf16[2,4,128,384]{2,3,1,0:T(8,128)(2,1)}, u32[]{:S(2)}, u32[]{:S(2)}) collective-permute-start(bf16[2,4,128,384]{2,3,1,0:T(8,128)(2,1)} %get-tuple-element.202), channel_id=1, source_target_pairs={{0,8},{8,0},{16,24},{24,16},{1,9},{9,1},{17,25},{25,17},{2,10},{10... | collective-permute-start | bytes 2359304 | tf_op jit(solution)/shard_map/ppermute | solution.py:72
  1007.0 60.1 %collective-permute-start.65 = (bf16[2,4,128,384]{2,3,1,0:T(8,128)(2,1)}, bf16[2,4,128,384]{2,3,1,0:T(8,128)(2,1)}, u32[]{:S(2)}, u32[]{:S(2)}) collective-permute-start(bf16[2,4,128,384]{2,3,1,0:T(8,128)(2,1)} %get-tuple-element.203), channel_id=1, source_target_pairs={{0,16},{8,24},{16,0},{24,8},{1,17},{9,25},{17,1},{25,9},{2,18},{10... | collective-permute-start | bytes 2359304 | tf_op jit(solution)/shard_map/ppermute | solution.py:72
  1012.9 54.1 %collective-permute-start.66 = (bf16[2,4,128,384]{2,3,1,0:T(8,128)(2,1)}, bf16[2,4,128,384]{2,3,1,0:T(8,128)(2,1)}, u32[]{:S(2)}, u32[]{:S(2)}) collective-permute-start(bf16[2,4,128,384]{2,3,1,0:T(8,128)(2,1)} %get-tuple-element.204), channel_id=1, source_target_pairs={{0,24},{8,16},{16,8},{24,0},{1,25},{9,17},{17,9},{25,1},{2,26},{10... | collective-permute-start | bytes 2359304 | tf_op jit(solution)/shard_map/ppermute | solution.py:72
  1017.3 46.4 %collective-permute-start.55 = (bf16[128,512]{1,0:T(8,128)(2,1)}, bf16[128,512]{1,0:T(8,128)(2,1)}, u32[]{:S(2)}, u32[]{:S(2)}) collective-permute-start(bf16[128,512]{1,0:T(8,128)(2,1)} %get-tuple-element.232), channel_id=1, source_target_pairs={{0,24},{8,16},{16,8},{24,0},{1,25},{9,17},{17,9},{25,1},{2,26},{10... | collective-permute-start | bytes 393224 | tf_op jit(solution)/shard_map/ppermute | solution.py:72
  1069.2 48.2 %collective-permute-start.67 = (bf16[4,4,128,384]{2,3,1,0:T(8,128)(2,1)S(1)}, bf16[4,4,128,384]{2,3,1,0:T(8,128)(2,1)S(1)}, u32[]{:S(2)}, u32[]{:S(2)}) collective-permute-start(bf16[4,4,128,384]{2,3,1,0:T(8,128)(2,1)S(1)} %get-tuple-element.199), channel_id=1, source_target_pairs={{0,1},{1,0},{2,3},{3,2},{4,5},{5,4},{6,7},{7,6},{8,9},{9,8},{10,11... | collective-permute-start | bytes 4718600 | tf_op jit(solution)/shard_map/ppermute | solution.py:72
  (193 other events, 3270.6 us)
Sparse Core Ops, SparseCore 0:
  782.1 131.4 all-reduce.1

commit v2 on v1

--- a/solution.py
+++ b/solution.py
@@ -88,6 +88,14 @@
     return lax.dynamic_index_in_dim(value, index, dim, keepdims=False)
 
 
+def total_sum(value):
+    for axis, mask in (("core", 1), ("x", 1), ("y", 1), ("z", 1), ("z", 2)):
+        value = value + partner(value, axis, mask)
+    if lax.axis_size("blk") > 1:
+        value = lax.psum(value, "blk")
+    return value
+
+
 def gather_tensor(own):
     across = partner(own, "x")
     beside = partner(own, "core")
@@ -106,91 +114,186 @@
     return lax.dot_general(left, right, (((1,), (1,)), ((), ())), preferred_element_type=F32)
 
 
-def expert_kernel(base, r0, r1, b0, b1, w, gu, gm, mixed, part, rows, back, acc_m, acc_p, acc_g):
+def tn_dot(left, right):
+    return lax.dot_general(left, right, (((0,), (0,)), ((), ())), preferred_element_type=F32)
+
+
+def spec(shape, index):
+    return pl.BlockSpec(shape, index)
+
+
+def assemble_kernel(offsets, *refs):
+    pieces, (wgu, wd) = refs[:8], refs[8:]
+    for k, piece in enumerate(pieces):
+        across, beside, far = k // 4, k // 2 % 2, k % 2
+        hidden = (beside * C + far) * LANES
+        for s in range(Z):
+            row = pl.multiple_of(offsets[s * Y + across], LANES)
+            wgu[0, pl.ds(row, LANES), hidden : hidden + LANES] = piece[s, 0, :LANES]
+            wgu[0, pl.ds(row, LANES), FF + hidden : FF + hidden + LANES] = piece[
+                s, 0, LANES : 2 * LANES
+            ]
+            wd[0, hidden : hidden + LANES, pl.ds(row, LANES)] = piece[s, 0, 2 * LANES :]
+
+
+def assemble(offsets, pieces):
+    count = pieces[0].shape[1]
+    return pl.pallas_call(
+        assemble_kernel,
+        grid_spec=pltpu.PrefetchScalarGridSpec(
+            num_scalar_prefetch=1,
+            grid=(count,),
+            in_specs=[spec((Z, 1, 3 * LANES, LANES), lambda i, o: (0, i, 0, 0))] * 8,
+            out_specs=[
+                spec((1, D, 2 * FF), lambda i, o: (i, 0, 0)),
+                spec((1, FF, D), lambda i, o: (i, 0, 0)),
+            ],
+        ),
+        out_shape=[
+            jax.ShapeDtypeStruct((count, D, 2 * FF), BF),
+            jax.ShapeDtypeStruct((count, FF, D), BF),
+        ],
+        compiler_params=pltpu.CompilerParams(vmem_limit_bytes=32 * 1024 * 1024),
+        cost_estimate=pl.CostEstimate(
+            flops=0, bytes_accessed=12 * count * D * FF, transcendentals=0
+        ),
+        name="assemble",
+    )(offsets, *pieces)
+
+
+def expert_kernel(first, chunk, half, experts, base, *refs):
+    if first:
+        r0, r1, b0, b1, wgu, wd = refs[:6]
+        refs = refs[6:] if chunk == 0 else refs[10:]
+        gu, gm, rows, back, mixed_out, part_out, acc_m, acc_p, acc_g = refs
+    else:
+        rows, back, wgu, wd, mixed_in, part_in = refs[:6]
+        refs = refs[6:] if chunk == 0 else refs[8:]
+        gu, gm, m0, m1, p0, p1, acc_m, acc_p, acc_g = refs
     i = pl.program_id(0)
-    half = r0.shape[0]
 
     @pl.when(i == 0)
     def _():
-        rows[:half, :] = r0[...]
-        rows[half:, :] = r1[...]
-        back[:half, :] = b0[...]
-        back[half:, :] = b1[...]
-        acc_m[...] = jnp.zeros_like(acc_m)
-        acc_p[...] = jnp.zeros_like(acc_p)
-        acc_g[...] = jnp.zeros_like(acc_g)
+        if first:
+            rows[:half, :] = r0[...]
+            rows[half:, :] = r1[...]
+            back[:half, :] = b0[...]
+            back[half:, :] = b1[...]
+            acc_m[...] = jnp.zeros_like(acc_m)
+            acc_p[...] = jnp.zeros_like(acc_p)
+            acc_g[...] = jnp.zeros_like(acc_g)
+        else:
+            acc_m[...] = mixed_in[...]
+            acc_p[...] = part_in[:, :D]
+            acc_g[...] = part_in[:, D:]
 
     expert = base[0] + i
-    mine = rows[:, :D]
-    gate_lanes = rows[:, D:].astype(F32)
-    lane = lax.broadcasted_iota(jnp.int32, gate_lanes.shape, 1)
-    wanted = (lane == expert) | (lane == expert + 32)
-    gate = jnp.sum(jnp.where(wanted, gate_lanes, 0.0), 1, keepdims=True)
-    wg = w[0, :, :FF]
-    wu = w[0, :, FF : 2 * FF]
-    wd = w[0, :, 2 * FF :]
-    gate_pre = jnp.dot(mine, wg, preferred_element_type=F32)
-    up_pre = jnp.dot(mine, wu, preferred_element_type=F32)
-    raw_back = jnp.dot(back[...], wd, preferred_element_type=F32)
-    sig = jax.nn.sigmoid(gate_pre)
-    active = gate_pre * sig
-    middle = (active * up_pre).astype(BF).astype(F32)
-    gate_grad = jnp.sum(middle * raw_back, 1, keepdims=True)
-    acc_g[...] += jnp.where(lane == expert, gate_grad, 0.0)
-    scaled = (gate * middle).astype(BF)
-    middle_back = gate * raw_back
-    gate_back = (middle_back * up_pre * sig * (1.0 + gate_pre * (1.0 - sig))).astype(BF)
-    up_back = (middle_back * active).astype(BF)
-    gu[:, :FF] = gate_back
-    gu[:, FF:] = up_back
-    gm[...] = scaled
-    acc_m[...] += nt_dot(scaled, wd)
-    acc_p[...] += nt_dot(gate_back, wg) + nt_dot(up_back, wu)
+    wg = wgu[0, :, :FF]
+    wu = wgu[0, :, FF:]
+    wdown = wd[0]
+    for t in range(2):
+        here = slice(t * half, (t + 1) * half)
+        mine = rows[here, :D]
+        gate_lanes = rows[here, D:].astype(F32)
+        lane = lax.broadcasted_iota(jnp.int32, gate_lanes.shape, 1)
+        wanted = (lane == expert) | (lane == expert + experts)
+        gate = jnp.sum(jnp.where(wanted, gate_lanes, 0.0), 1, keepdims=True)
+        gate_pre = jnp.dot(mine, wg, preferred_element_type=F32)
+        up_pre = jnp.dot(mine, wu, preferred_element_type=F32)
+        raw_back = nt_dot(back[here, :], wdown)
+        sig = jax.nn.sigmoid(gate_pre)
+        active = gate_pre * sig
+        middle = (active * up_pre).astype(BF).astype(F32)
+        gate_grad = jnp.sum(middle * raw_back, 1, keepdims=True)
+        acc_g[here, :] += jnp.where(lane == expert, gate_grad, 0.0)
+        scaled = (gate * middle).astype(BF)
+        middle_back = gate * raw_back
+        gate_back = (middle_back * up_pre * (sig + active * (1.0 - sig))).astype(BF)
+        up_back = (middle_back * active).astype(BF)
+        gu[here, :FF] = gate_back
+        gu[here, FF:] = up_back
+        gm[here, :] = scaled
+        acc_m[here, :] += jnp.dot(scaled, wdown, preferred_element_type=F32)
+        acc_p[here, :] += nt_dot(gate_back, wg) + nt_dot(up_back, wu)
 
     @pl.when(i == pl.num_programs(0) - 1)
     def _():
-        mixed[...] = acc_m[...].astype(BF)
-        part[:, :D] = acc_p[...].astype(BF)
-        part[:, D:] = acc_g[...].astype(BF)
-
-
-def expert_chunk(base, r0, r1, b0, b1, weights):
-    together = weights.shape[0]
-    half, wide = r0.shape
+        if first:
+            mixed_out[...] = acc_m[...]
+            part_out[:, :D] = acc_p[...]
+            part_out[:, D:] = acc_g[...]
+        else:
+            m0[...] = acc_m[:half, :].astype(BF)
+            m1[...] = acc_m[half:, :].astype(BF)
+            p0[:, :D] = acc_p[:half, :].astype(BF)
+            p0[:, D:] = acc_g[:half, :].astype(BF)
+            p1[:, :D] = acc_p[half:, :].astype(BF)
+            p1[:, D:] = acc_g[half:, :].astype(BF)
+
+
+def expert_chunk(first, chunk, half, experts, base, tokens, weights, carried, sums):
+    wgu, wd = weights
+    together = wgu.shape[0]
     count = 2 * half
+    wide = D + LANES
     whole = lambda i, s: (0, 0)
+    at_chunk = lambda i, s: (chunk, 0)
+    at_both = lambda i, s: (chunk, i)
+    weight_specs = [
+        spec((1, D, 2 * FF), lambda i, s: (i, 0, 0)),
+        spec((1, FF, D), lambda i, s: (i, 0, 0)),
+    ]
+    any_spec = pl.BlockSpec(memory_space=pl.ANY)
+    shape = jax.ShapeDtypeStruct
+    hidden_specs = [spec((count, 2 * FF), at_both), spec((count, FF), at_both)]
+    hidden_shapes = [
+        shape((Z * count, together * 2 * FF), BF),
+        shape((Z * count, together * FF), BF),
+    ]
+    if first:
+        in_specs = [spec((half, wide), whole)] * 2 + [spec((half, D), whole)] * 2 + weight_specs
+        operands = list(tokens) + [wgu, wd]
+        out_specs = hidden_specs + [
+            spec((count, wide), at_chunk),
+            spec((count, D), at_chunk),
+            spec((count, D), whole),
+            spec((count, wide), whole),
+        ]
+        out_shape = hidden_shapes + [
+            shape((Z * count, wide), BF),
+            shape((Z * count, D), BF),
+            shape((count, D), F32),
+            shape((count, wide), F32),
+        ]
+    else:
+        in_specs = (
+            [spec((count, wide), at_chunk), spec((count, D), at_chunk)]
+            + weight_specs
+            + [spec((count, D), whole), spec((count, wide), whole)]
+        )
+        operands = list(tokens) + [wgu, wd] + list(sums)
+        out_specs = hidden_specs + [spec((half, D), whole)] * 2 + [spec((half, wide), whole)] * 2
+        out_shape = hidden_shapes + [shape((half, D), BF)] * 2 + [shape((half, wide), BF)] * 2
+    aliases = {}
+    if chunk > 0:
+        aliases = {1 + len(operands) + k: k for k in range(len(carried))}
+        in_specs = in_specs + [any_spec] * len(carried)
+        operands = operands + list(carried)
     return pl.pallas_call(
-        expert_kernel,
+        lambda *refs: expert_kernel(first, chunk, half, experts, *refs),
         grid_spec=pltpu.PrefetchScalarGridSpec(
             num_scalar_prefetch=1,
             grid=(together,),
-            in_specs=[
-                pl.BlockSpec((half, wide), whole),
-                pl.BlockSpec((half, wide), whole),
-                pl.BlockSpec((half, D), whole),
-                pl.BlockSpec((half, D), whole),
-                pl.BlockSpec((1, D, 3 * FF), lambda i, s: (i, 0, 0)),
-            ],
-            out_specs=[
-                pl.BlockSpec((count, 2 * FF), lambda i, s: (0, i)),
-                pl.BlockSpec((count, FF), lambda i, s: (0, i)),
-                pl.BlockSpec((count, D), whole),
-                pl.BlockSpec((count, wide), whole),
-            ],
+            in_specs=in_specs,
+            out_specs=out_specs,
             scratch_shapes=[
-                pltpu.VMEM((count, wide), BF),
-                pltpu.VMEM((count, D), BF),
                 pltpu.VMEM((count, D), F32),
                 pltpu.VMEM((count, D), F32),
                 pltpu.VMEM((count, LANES), F32),
             ],
         ),
-        out_shape=[
-            jax.ShapeDtypeStruct((count, together * 2 * FF), BF),
-            jax.ShapeDtypeStruct((count, together * FF), BF),
-            jax.ShapeDtypeStruct((count, D), BF),
-            jax.ShapeDtypeStruct((count, wide), BF),
-        ],
+        out_shape=out_shape,
+        input_output_aliases=aliases,
         compiler_params=pltpu.CompilerParams(vmem_limit_bytes=48 * 1024 * 1024),
         cost_estimate=pl.CostEstimate(
             flops=12 * together * count * D * FF,
@@ -198,7 +301,112 @@
             transcendentals=together * count * FF,
         ),
         name="experts",
-    )(base, r0, r1, b0, b1, weights)
+    )(base, *operands)
+
+
+def grad_kernel(offsets, rows, back, gu, gm, keep_a, send_a, keep_b, send_b, hidden, down):
+    hidden[...] = tn_dot(rows[:, :D], gu[...]).astype(BF)
+    down[...] = tn_dot(gm[...], back[...]).astype(BF)
+    for s in range(Z):
+        for across in range(Y):
+            row = pl.multiple_of(offsets[s * Y + across], LANES)
+            for beside in range(X):
+                for far in range(C):
+                    at = (beside * C + far) * LANES
+                    if far == 0:
+                        target = (keep_a, send_a)[across].at[s, beside, 0]
+                    else:
+                        target = (keep_b, send_b)[beside].at[s, across, 0]
+                    target[:LANES, :] = hidden[pl.ds(row, LANES), at : at + LANES]
+                    target[LANES : 2 * LANES, :] = hidden[
+                        pl.ds(row, LANES), FF + at : FF + at + LANES
+                    ]
+                    target[2 * LANES :, :] = down[at : at + LANES, pl.ds(row, LANES)]
+
+
+def expert_grads(offsets, rows, back, gu, gm):
+    count = rows.shape[0]
+    together = gm.shape[1] // FF
+    piece = spec((Z, 2, 1, 3 * LANES, LANES), lambda i, o: (0, 0, i, 0, 0))
+    whole = lambda i, o: (0, 0)
+    return pl.pallas_call(
+        grad_kernel,
+        grid_spec=pltpu.PrefetchScalarGridSpec(
+            num_scalar_prefetch=1,
+            grid=(together,),
+            in_specs=[
+                spec((count, D + LANES), whole),
+                spec((count, D), whole),
+                spec((count, 2 * FF), lambda i, o: (0, i)),
+                spec((count, FF), lambda i, o: (0, i)),
+            ],
+            out_specs=[piece] * 4,
+            scratch_shapes=[pltpu.VMEM((D, 2 * FF), BF), pltpu.VMEM((FF, D), BF)],
+        ),
+        out_shape=[jax.ShapeDtypeStruct((Z, 2, together, 3 * LANES, LANES), BF)] * 4,
+        compiler_params=pltpu.CompilerParams(vmem_limit_bytes=56 * 1024 * 1024),
+        cost_estimate=pl.CostEstimate(
+            flops=6 * together * count * D * FF,
+            bytes_accessed=4 * count * D + 12 * together * D * FF,
+            transcendentals=0,
+        ),
+        name="expert_grads",
+    )(offsets, rows, back, gu, gm)
+
+
+def adam_kernel(rate_wide, rate_down, table, grad, *refs):
+    ins, outs = refs[:6], refs[6:]
+    for k in range(2):
+        new = adam_update(
+            ins[0][k],
+            grad[0, 0, :, k * LANES : (k + 1) * LANES, :].astype(F32),
+            ins[1][k],
+            ins[2][k],
+            rate_wide,
+            WEIGHT_DECAY,
+        )
+        for ref, value in zip(outs[:3], new):
+            ref[k] = value
+    new = adam_update(
+        ins[3][...],
+        grad[0, 0, :, 2 * LANES :, :].astype(F32),
+        ins[4][...],
+        ins[5][...],
+        rate_down,
+        WEIGHT_DECAY,
+    )
+    for ref, value in zip(outs[3:], new):
+        ref[...] = value
+
+
+def expert_adam(table, grads, gate_up, down, rate_wide, rate_down):
+    together = grads.shape[2]
+    two = spec((2, together, LANES, LANES), lambda g, t: (0, g, 0, 0))
+    one = spec((together, LANES, LANES), lambda g, t: (g, 0, 0))
+    return pl.pallas_call(
+        lambda *refs: adam_kernel(rate_wide, rate_down, *refs),
+        grid_spec=pltpu.PrefetchScalarGridSpec(
+            num_scalar_prefetch=1,
+            grid=(Z * C,),
+            in_specs=[
+                spec(
+                    (1, 1, together, 3 * LANES, LANES),
+                    lambda g, t: (t[2 * g], t[2 * g + 1], 0, 0, 0),
+                )
+            ]
+            + [two] * 3
+            + [one] * 3,
+            out_specs=[two] * 3 + [one] * 3,
+        ),
+        out_shape=[jax.ShapeDtypeStruct(v.shape, F32) for v in gate_up + down],
+        compiler_params=pltpu.CompilerParams(vmem_limit_bytes=40 * 1024 * 1024),
+        cost_estimate=pl.CostEstimate(
+            flops=20 * 3 * grads.size,
+            bytes_accessed=26 * grads.size,
+            transcendentals=grads.size,
+        ),
+        name="expert_adam",
+    )(table, grads, *gate_up, *down)
 
 
 def body(
@@ -276,35 +484,50 @@
     back_z = [back_own] + [partner(back_own, "z", s) for s in range(1, Z)]
     back_pairs = [(v, partner(v, "core")) for v in back_z]
 
-    expert_own = jnp.concatenate(
-        [gate_up_weight[0], gate_up_weight[1], down_weight.transpose(0, 2, 1)], 2
-    ).astype(BF)
-    expert_wide = expert_own.shape[2]
+    gate_up_low, down_low = gate_up_weight.astype(BF), down_weight.astype(BF)
     if blocks > 1:
-        expert_own = lax.all_gather(expert_own, "blk", axis=1, tiled=True)
-    expert_own = expert_own.reshape(Z, C, together, deep, expert_wide)
+        gate_up_low = lax.all_gather(gate_up_low, "blk", axis=2, tiled=True)
+        down_low = lax.all_gather(down_low, "blk", axis=2, tiled=True)
+    expert_own = jnp.concatenate([gate_up_low[0], gate_up_low[1], down_low], 1)
+    expert_own = expert_own.reshape(Z, C, together, 3 * LANES, LANES)
     kept = pick(expert_own, c, 1)
     moved = partner(pick(expert_own, 1 - c, 1), "core")
-    both = jnp.stack([kept, moved])
-    from_z = [pick(both, z, 1)] + [
-        partner(pick(both, z ^ s, 1), "z", s) for s in range(1, Z)
-    ]
-    pieces = jnp.stack(from_z, 1)
-    here = [[None, None], [None, None]]
-    piece_a, piece_b = pieces[0], pieces[1]
-    a_x = partner(piece_a, "x")
-    b_y = partner(piece_b, "y")
-    grid_a = jnp.stack(
-        [jnp.stack([piece_a, a_x]), jnp.stack([partner(piece_a, "y"), partner(a_x, "y")])]
-    )
-    grid_b = jnp.stack(
-        [jnp.stack([piece_b, partner(piece_b, "x")]), jnp.stack([b_y, partner(b_y, "x")])]
-    )
-    grid = jnp.stack([grid_a, grid_b], 3).reshape(
-        Y, X, Z, C, together, blocks, depth, 3, expert_wide // 3
-    )
-    grid = to_absolute(to_absolute(grid, "y", 0), "z", 2)
-    expert_weights = grid.transpose(4, 5, 2, 0, 6, 7, 1, 3, 8).reshape(together, D, 3 * FF)
+    offsets = jnp.stack(
+        [((z ^ s) * Y + (y ^ k)) * LANES for s in range(Z) for k in range(Y)]
+    ).astype(jnp.int32)
+    halves = 2
+    per_half = together // halves
+    half_weights = []
+    for h in range(halves):
+        span = slice(h * per_half, (h + 1) * per_half)
+        near = [pick(kept[:, span], z, 0)]
+        far = [pick(moved[:, span], z, 0)]
+        for s in range(1, Z):
+            got = partner(
+                jnp.stack([pick(kept[:, span], z ^ s, 0), pick(moved[:, span], z ^ s, 0)]), "z", s
+            )
+            near.append(got[0])
+            far.append(got[1])
+        near, far = jnp.stack(near), jnp.stack(far)
+        near_x = partner(near, "x")
+        far_y = partner(far, "y")
+        pieces = [
+            near,
+            far,
+            near_x,
+            partner(far, "x"),
+            partner(near, "y"),
+            far_y,
+            partner(near_x, "y"),
+            partner(far_y, "x"),
+        ]
+        wgu, wd = assemble(offsets, pieces)
+        if blocks > 1:
+            wgu = wgu.reshape(per_half, Z * Y, blocks, depth, 2 * FF)
+            wgu = wgu.transpose(0, 2, 1, 3, 4).reshape(per_half, D, 2 * FF)
+            wd = wd.reshape(per_half, FF, Z * Y, blocks, depth)
+            wd = wd.transpose(0, 1, 3, 2, 4).reshape(per_half, FF, D)
+        half_weights.append((wgu, wd))
 
     qkv_raw = jnp.dot(rows_one, qkv_full, preferred_element_type=F32)
     queries = (
@@ -376,72 +599,83 @@
     rows_z = [rows_own] + [partner(rows_own, "z", s) for s in range(1, Z)]
     rows_pairs = [(v, partner(v, "core")) for v in rows_z]
     base = ((z * C + c) * together).astype(jnp.int32).reshape(1)
-    hidden_parts = []
-    down_parts = []
-    mixed_total = None
-    back_total = None
+    sums = []
+    carried = ()
     for s in range(Z):
-        gu, gm, mixed, part = expert_chunk(base, *rows_pairs[s], *back_pairs[s], expert_weights)
-        hidden_parts.append(gu)
-        down_parts.append(gm)
-        part_sum = part[:local_rows].astype(F32) + partner(part[local_rows:], "core").astype(F32)
-        mixed_sum = mixed[:local_rows].astype(F32) + partner(mixed[local_rows:], "core").astype(F32)
+        out = expert_chunk(
+            True,
+            s,
+            local_rows,
+            experts,
+            base,
+            rows_pairs[s] + back_pairs[s],
+            half_weights[0],
+            carried,
+            None,
+        )
+        carried = out[:4]
+        sums.append(out[4:])
+    rows_all, back_all = carried[2:]
+
+    def to_pieces(rows):
+        if blocks == 1:
+            return rows
+        own = rows[:, :D].reshape(-1, blocks, Z * Y, depth).transpose(0, 2, 1, 3)
+        return jnp.concatenate([own.reshape(-1, D), rows[:, D:]], 1)
+
+    def expert_sums(gu, gm):
+        keep_a, send_a, keep_b, send_b = expert_grads(
+            offsets, to_pieces(rows_all), to_pieces(back_all), gu, gm
+        )
+        sum_a = (keep_a.astype(F32) + partner(send_a, "y").astype(F32)).astype(BF)
+        sum_b = (keep_b.astype(F32) + partner(send_b, "x").astype(F32)).astype(BF)
+        total_a = sum_a[:, 0].astype(F32) + partner(sum_a[:, 1], "x").astype(F32)
+        total_b = sum_b[:, 0].astype(F32) + partner(sum_b[:, 1], "y").astype(F32)
+        total = jnp.stack([total_a, total_b], 1).astype(BF)
+        owned = jnp.stack([total[0]] + [partner(total[s], "z", s) for s in range(1, Z)])
+        return owned[:, 0], partner(owned[:, 1], "core")
+
+    owned = [expert_sums(*carried[:2])]
+    carried = ()
+    back_total, mixed_parts = None, []
+    for s in range(Z):
+        out = expert_chunk(
+            False,
+            s,
+            local_rows,
+            experts,
+            base + per_half,
+            (rows_all, back_all),
+            half_weights[1],
+            carried,
+            sums[s],
+        )
+        carried = out[:2]
+        m0, m1, p0, p1 = out[2:]
+        part_sum = p0.astype(F32) + partner(p1, "core").astype(F32)
+        mixed_parts.append((m0, m1))
         if s == 0:
-            back_total, mixed_total = part_sum, mixed_sum
+            back_total = part_sum
         else:
             back_total = back_total + partner(part_sum.astype(BF), "z", s).astype(F32)
+    owned.append(expert_sums(*carried))
+    mixed_total = None
+    for s in range(Z):
+        m0, m1 = mixed_parts[s]
+        mixed_sum = m0.astype(F32) + partner(m1, "core").astype(F32)
+        if s == 0:
+            mixed_total = mixed_sum
+        else:
             mixed_total = mixed_total + partner(mixed_sum.astype(BF), "z", s).astype(F32)
     result = hidden + mixed_total
-
-    rows_all = jnp.concatenate([v[:, :D] for pair in rows_pairs for v in pair], 0)
-    back_all = jnp.concatenate([v for pair in back_pairs for v in pair], 0)
-    hidden_grad = lax.dot_general(
-        rows_all,
-        jnp.concatenate(hidden_parts, 0),
-        (((0,), (0,)), ((), ())),
-        preferred_element_type=F32,
-    ).astype(BF)
-    down_grad = lax.dot_general(
-        back_all,
-        jnp.concatenate(down_parts, 0),
-        (((0,), (0,)), ((), ())),
-        preferred_element_type=F32,
-    ).astype(BF)
-    lane_wide = expert_wide // 3
-    grads = jnp.concatenate(
-        [
-            hidden_grad.reshape(blocks, Z, Y, depth, together, 2, X, C, lane_wide),
-            down_grad.reshape(blocks, Z, Y, depth, together, 1, X, C, lane_wide),
-        ],
-        5,
-    )
-    grads = grads.transpose(7, 6, 2, 1, 4, 0, 3, 5, 8).reshape(
-        C, X, Y, Z, together, deep, expert_wide
-    )
-    grads_a, grads_b = grads[0], grads[1]
-    keep_a = pick(grads_a, y, 1).astype(F32)
-    got_a = partner(pick(grads_a, 1 - y, 1), "y").astype(F32)
-    sum_a = keep_a + got_a
-    total_a = sum_a[0] + partner(sum_a[1].astype(BF), "x").astype(F32)
-    sum_b = grads_b[0].astype(F32) + partner(grads_b[1], "x").astype(F32)
-    total_b = pick(sum_b, y, 0) + partner(pick(sum_b, 1 - y, 0).astype(BF), "y").astype(F32)
-    totals = jnp.stack([total_a, total_b]).astype(BF)
-    owned_z = jnp.stack(
-        [pick(totals, z, 1)] + [partner(pick(totals, z ^ s, 1), "z", s) for s in range(1, Z)], 1
-    )
-    owned = jnp.stack([owned_z[0], partner(owned_z[1], "core")], 1)
-    owned = to_absolute(to_absolute(owned, "core", 1), "z", 0)
-    owned = owned.reshape(experts, deep, expert_wide)
-    if blocks > 1:
-        owned = lax.psum_scatter(owned.astype(F32), "blk", scatter_dimension=1, tiled=True)
-    owned = owned.reshape(experts, depth, 3, lane_wide).astype(F32)
-    gate_up_grad = jnp.stack([owned[:, :, 0], owned[:, :, 1]])
-    down_owned = owned[:, :, 2].transpose(0, 2, 1)
+    owned = jnp.stack([jnp.concatenate([h[k] for h in owned], 1) for k in range(C)])
 
     expert_part = back_total[:, :D]
     gate_grad = back_total[:, D : D + experts]
     logit_back = gates * (gate_grad - jnp.sum(gates * gate_grad, -1, keepdims=True))
-    router_part = jnp.dot(normed_two.astype(F32).T, logit_back, precision=HIGH)
+    router_part = lax.dot_general(
+        logit_back, normed_two.astype(F32), (((0,), (0,)), ((), ())), precision=HIGH
+    )
     normed_two_back = expert_part + jnp.dot(logit_back, router_low.astype(F32).T, precision=HIGH)
     unit_two = hidden * scale_two
     weighted_two = normed_two_back * norm_gains[1]
@@ -490,12 +724,13 @@
     normed_one_back = scatter_tensor(
         [normed_part[b * local_rows : (b + 1) * local_rows] for b in range(X * C)]
     )
+    gain_one = jnp.sum(normed_part * rows_one.astype(F32), 0, keepdims=True)
+    gain_one = total_sum(gain_one) / norm_gains[:1]
     unit_one = stream * scale_one
     weighted_one = normed_one_back * norm_gains[0]
     stream_grad = hidden_back + scale_one * (
         weighted_one - unit_one * jnp.mean(weighted_one * unit_one, -1, keepdims=True)
     )
-    gain_one = jnp.sum(normed_one_back * unit_one, 0)
 
     def data_scatter(grad):
         wide = grad.shape[1]
@@ -513,12 +748,9 @@
     qkv_owned = data_scatter(qkv_grad)
     query_owned = qkv_owned[:, :query_wide]
     pair_owned = jnp.stack([qkv_owned[:, query_wide:first_pair], qkv_owned[:, first_pair:]])
-    gain_two, router_grad = lax.psum((gain_part_two, router_part), EVERY)
-    for axis, mask in (("core", 1), ("x", 1), ("y", 1), ("z", 1), ("z", 2)):
-        gain_one = gain_one + partner(gain_one, axis, mask)
-    if blocks > 1:
-        gain_one = lax.psum(gain_one, "blk")
-    gain_grad = jnp.stack([gain_one, gain_two])
+    small = total_sum(jnp.concatenate([router_part, gain_part_two[None, :]], 0))
+    router_grad = small[:experts].T
+    gain_grad = jnp.concatenate([gain_one, small[experts:]], 0)
     rate_wide = 2.0 * D ** (-0.5)
     rate_output = 2.0 * max(1, 2 * H * HD // group_rows) ** (-0.5)
     rate_router = 2.0 * (4 * D) ** (-0.5)
@@ -535,12 +767,32 @@
     router_new = adam_update(
         router_weight, router_grad, router_moment, router_second, rate_router, WEIGHT_DECAY
     )
-    gate_up_new = adam_update(
-        gate_up_weight, gate_up_grad, gate_up_moment, gate_up_second, rate_wide, WEIGHT_DECAY
-    )
-    down_new = adam_update(
-        down_weight, down_owned, down_moment, down_second, rate_down, WEIGHT_DECAY
-    )
+    if blocks == 1:
+        table = jnp.stack(
+            [v for k in range(Z * C) for v in ((k % C) ^ c, (k // C) ^ z)]
+        ).astype(jnp.int32)
+        expert_new = expert_adam(
+            table,
+            owned,
+            [gate_up_weight, gate_up_moment, gate_up_second],
+            [down_weight, down_moment, down_second],
+            rate_wide,
+            rate_down,
+        )
+        gate_up_new, down_new = tuple(expert_new[:3]), tuple(expert_new[3:])
+    else:
+        placed = to_absolute(to_absolute(owned, "core", 0), "z", 1).transpose(1, 0, 2, 3, 4)
+        placed = placed.reshape(experts, 3, LANES, LANES).astype(F32)
+        gate_up_grad = lax.psum_scatter(
+            placed[:, :2].transpose(1, 0, 2, 3), "blk", scatter_dimension=2, tiled=True
+        )
+        down_grad = lax.psum_scatter(placed[:, 2], "blk", scatter_dimension=2, tiled=True)
+        gate_up_new = adam_update(
+            gate_up_weight, gate_up_grad, gate_up_moment, gate_up_second, rate_wide, WEIGHT_DECAY
+        )
+        down_new = adam_update(
+            down_weight, down_grad, down_moment, down_second, rate_down, WEIGHT_DECAY
+        )
     gains_new = adam_update(norm_gains, gain_grad, gains_moment, gains_second, 0.2, 0.0)
     return (
         (result, stream_grad)

time: 1180 us -> 870 us (0.74)
  local copies, waits for them, and re-layouts: 275 us -> 60.8 us
  blocking collectives: 110 us -> 0 us
  Pallas kernels: 78.2 us -> 174 us
  other arithmetic: 154 us -> 71 us
  matrix products: 84.2 us -> 42.2 us
  starting transfers between devices: 94.5 us -> 126 us
  waiting for transfers between devices: 352 us -> 383 us
  between operations: 17.2 us -> 3.72 us
    psum x1 -> x0, blocking collectives: 110 us -> none  [body(): gain_two, router_grad = lax.psum((gain_part_two, router_part), EVERY)]
    pallas_call x4 -> x13, Pallas kernels: 78.2 us -> 174 us  [the longest x8 106 us: expert_chunk(): pl.pallas_call(lambda *refs: expert_kernel(first, chunk, half, experts, *...]
    reshape x5 -> x0, local copies, waits for them, and re-layouts: 81.6 us -> none  [the longest x2 35.4 us: body(): hidden_grad.reshape(blocks, Z, Y, depth, together, 2, X, C, lane_wide)]
    unnamed x327 -> x288, local copies, waits for them, and re-layouts: 71.8 us -> 33.5 us
    dot_general x3 -> x1, matrix products: 38.9 us -> 0.54 us  [body(): lax.dot_general(logit_back, normed_two.astype(F32), (((0,), (0,)), ((), (...]
    ppermute x73 -> x95, waiting for transfers between devices: 351 us -> 383 us  [partner(): return lax.ppermute(value, axis, [(i, i ^ mask) for i in range(size)])]
    transpose x1 -> x0, local copies, waits for them, and re-layouts: 31.3 us -> none  [body(): grid.transpose(4, 5, 2, 0, 6, 7, 1, 3, 8).reshape(together, D, 3 * FF)]
    ppermute x73 -> x95, starting transfers between devices: 94.5 us -> 126 us  [partner(): return lax.ppermute(value, axis, [(i, i ^ mask) for i in range(size)])]
  transfers between devices with their start and end apart: 74 -> 95, of which waited for: 23 -> 33; matrix products, arithmetic and copies ran while one was open for 27% -> 17% of each run, Pallas kernels for 5% -> 13%
where the time goes in v2:
time: 870 us; the launch traced here: 861 us
  waiting for transfers between devices  383 us (44%)
  Pallas kernels  174 us (20%)
  starting transfers between devices  126 us (14%)
  other arithmetic  71 us (8%)
  local copies, waits for them, and re-layouts  60.8 us (7%)
  matrix products  42.2 us (5%)
    ppermute x95, waiting for transfers between devices, partner(): return lax.ppermute(value, axis, [(i, i ^ mask) for i in range(size)])  383 us
    ppermute x95, starting transfers between devices, partner(): return lax.ppermute(value, axis, [(i, i ^ mask) for i in range(size)])  126 us
    pallas_call x8, Pallas kernels, expert_chunk(): pl.pallas_call(lambda *refs: expert_kernel(first, chunk, half, experts, *...  106 us
    pallas_call x2, Pallas kernels, expert_grads(): pl.pallas_call(grad_kernel, grid_spec=pltpu.PrefetchScalarGridSpec(num_sc...  45.7 us
    unnamed x288, local copies, waits for them, and re-layouts  33.5 us
  transfers between devices with their start and end apart: 95, of which 33 were waited for; matrix products, arithmetic and copies ran while one was open for 17% of the time, Pallas kernels for 13%

profile of v2, /device:TPU:0, one launch (start us, length us, event | category | flops | bytes accessed | tf_op | source)
XLA Modules:
  0.0 860.5 jit_solution(12658677411145715013)
XLA Ops:
  36.1 15.6 %collective-permute-done.6 = bf16[4,128,768]{2,1,0:T(8,128)(2,1)S(1)} collective-permute-done((bf16[4,128,768]{2,1,0:T(8,128)(2,1)}, bf16[4,128,768]{2,1,0:T(8,128)(2,1)S(1)}, u32[]{:S(2)}, u32[]{:S(2)}) %collective-permute-start.6) | collective-permute-done | bytes 786464 | tf_op jit(solution)/shard_map/ppermute | solution.py:72
  86.2 17.1 %collective-permute-start.34 = (bf16[2,2,384,128]{3,2,1,0:T(8,128)(2,1)S(1)}, bf16[2,2,384,128]{3,2,1,0:T(8,128)(2,1)S(1)}, u32[]{:S(2)}, u32[]{:S(2)}) collective-permute-start(bf16[2,2,384,128]{3,2,1,0:T(8,128)(2,1)S(1)} %pad_maximum_fusion.25), channel_id=1, source_target_pairs={{0,16},{8,24},{16,0},{24,8},{1,17},{9,25},{17,1},{25,9},{2,18},{10... | collective-permute-start | bytes 1179656 | tf_op jit(solution)/shard_map/ppermute | solution.py:72
  103.3 23.8 %collective-permute-done.15 = bf16[2,2,384,128]{3,2,1,0:T(8,128)(2,1)S(1)} collective-permute-done((bf16[2,2,384,128]{3,2,1,0:T(8,128)(2,1)S(1)}, bf16[2,2,384,128]{3,2,1,0:T(8,128)(2,1)S(1)}, u32[]{:S(2)}, u32[]{:S(2)}) %collective-permute-start.15) | collective-permute-done | bytes 393248 | tf_op jit(solution)/shard_map/ppermute | solution.py:72
  131.6 12.1 %collective-permute-done.34 = bf16[2,2,384,128]{3,2,1,0:T(8,128)(2,1)S(1)} collective-permute-done((bf16[2,2,384,128]{3,2,1,0:T(8,128)(2,1)S(1)}, bf16[2,2,384,128]{3,2,1,0:T(8,128)(2,1)S(1)}, u32[]{:S(2)}, u32[]{:S(2)}) %collective-permute-start.34) | collective-permute-done | bytes 393248 | tf_op jit(solution)/shard_map/ppermute | solution.py:72
  148.5 25.7 %collective-permute-done.8 = bf16[256,1024]{1,0:T(8,128)(2,1)S(1)} collective-permute-done((bf16[256,1024]{1,0:T(8,128)(2,1)S(1)}, bf16[256,1024]{1,0:T(8,128)(2,1)S(1)}, u32[]{:S(2)}, u32[]{:S(2)}) %collective-permute-start.8) | collective-permute-done | bytes 524320 | tf_op jit(solution)/shard_map/ppermute | solution.py:72
  182.1 26.9 %collective-permute-done.36.refs_2_ = bf16[4,2,384,128]{3,2,1,0:T(8,128)(2,1)} collective-permute-done((bf16[4,2,384,128]{3,2,1,0:T(8,128)(2,1)}, bf16[4,2,384,128]{3,2,1,0:T(8,128)(2,1)}, u32[]{:S(2)}, u32[]{:S(2)}) %collective-permute-start.36) | collective-permute-done | bytes 786464 | tf_op jit(solution)/shard_map/ppermute | solution.py:72
  218.4 10.6 %collective-permute-done.21.refs_6_ = bf16[4,2,384,128]{3,2,1,0:T(8,128)(2,1)} collective-permute-done((bf16[4,2,384,128]{3,2,1,0:T(8,128)(2,1)}, bf16[4,2,384,128]{3,2,1,0:T(8,128)(2,1)}, u32[]{:S(2)}, u32[]{:S(2)}) %collective-permute-start.21) | collective-permute-done | bytes 786464 | tf_op jit(solution)/shard_map/ppermute | solution.py:72
  233.5 9.5 %collective-permute-done.40.refs_6_ = bf16[4,2,384,128]{3,2,1,0:T(8,128)(2,1)} collective-permute-done((bf16[4,2,384,128]{3,2,1,0:T(8,128)(2,1)}, bf16[4,2,384,128]{3,2,1,0:T(8,128)(2,1)}, u32[]{:S(2)}, u32[]{:S(2)}) %collective-permute-start.40) | collective-permute-done | bytes 786464 | tf_op jit(solution)/shard_map/ppermute | solution.py:72
  271.6 13.4 %experts.8 = (bf16[2048,2048]{1,0:T(8,128)(2,1)}, bf16[2048,1024]{1,0:T(8,128)(2,1)}, bf16[2048,1152]{1,0:T(8,128)(2,1)}, bf16[2048,1024]{1,0:T(8,128)(2,1)}, f3...) custom-call(s32[1]{0:T(128)} %bitcast.37.refs_0_, bf16[256,1152]{1,0:T(8,128)(2,1)S(1)} %concatenate.121.refs_1_, ...), custom_call_target="tpu_custom_call" | custom-call | flops 6442450944 | bytes 14680064 | tf_op jit(solution)/shard_map/experts/pallas_call | solution.py:282
  286.3 32.7 %collective-permute-done.25.refs_3_ = bf16[256,1024]{1,0:T(8,128)(2,1)S(1)} collective-permute-done((bf16[256,1024]{1,0:T(8,128)(2,1)}, bf16[256,1024]{1,0:T(8,128)(2,1)S(1)}, u32[]{:S(2)}, u32[]{:S(2)}) %collective-permute-start.25) | collective-permute-done | bytes 524320 | tf_op jit(solution)/shard_map/ppermute | solution.py:72
  319.6 24.6 %collective-permute-done.23.refs_1_ = bf16[256,1152]{1,0:T(8,128)(2,1)S(1)} collective-permute-done((bf16[256,1152]{1,0:T(8,128)(2,1)S(1)}, bf16[256,1152]{1,0:T(8,128)(2,1)S(1)}, u32[]{:S(2)}, u32[]{:S(2)}) %collective-permute-start.23) | collective-permute-done | bytes 589856 | tf_op jit(solution)/shard_map/ppermute | solution.py:72
  344.2 13.2 %experts.9 = (bf16[2048,2048]{1,0:T(8,128)(2,1)}, bf16[2048,1024]{1,0:T(8,128)(2,1)}, bf16[2048,1152]{1,0:T(8,128)(2,1)}, bf16[2048,1024]{1,0:T(8,128)(2,1)}, f3...) custom-call(s32[1]{0:T(128)} %bitcast.37.refs_0_, ...), custom_call_target="tpu_custom_call", output_to_operand_aliasing={{0}: (7, {}), {1}: (8, {}), {2}: (9, {}), {3}: (10, {})} | custom-call | flops 6442450944 | bytes 14680064 | tf_op jit(solution)/shard_map/experts/pallas_call | solution.py:282
  358.7 13.0 %experts.10 = (bf16[2048,2048]{1,0:T(8,128)(2,1)}, bf16[2048,1024]{1,0:T(8,128)(2,1)}, bf16[2048,1152]{1,0:T(8,128)(2,1)}, bf16[2048,1024]{1,0:T(8,128)(2,1)}, f...) custom-call(s32[1]{0:T(128)} %bitcast.37.refs_0_, ...), custom_call_target="tpu_custom_call", output_to_operand_aliasing={{0}: (7, {}), {1}: (8, {}), {2}: (9, {}), {3}: (10, {})} | custom-call | flops 6442450944 | bytes 14680064 | tf_op jit(solution)/shard_map/experts/pallas_call | solution.py:282
  373.1 13.6 %experts.11 = (bf16[2048,2048]{1,0:T(8,128)(2,1)}, bf16[2048,1024]{1,0:T(8,128)(2,1)}, bf16[2048,1152]{1,0:T(8,128)(2,1)}, bf16[2048,1024]{1,0:T(8,128)(2,1)}, f...) custom-call(s32[1]{0:T(128)} %bitcast.37.refs_0_, ...), custom_call_target="tpu_custom_call", output_to_operand_aliasing={{0}: (7, {}), {1}: (8, {}), {2}: (9, {}), {3}: (10, {})} | custom-call | flops 6442450944 | bytes 14680064 | tf_op jit(solution)/shard_map/experts/pallas_call | solution.py:282
  388.0 12.9 %experts.12 = (bf16[2048,2048]{1,0:T(8,128)(2,1)}, bf16[2048,1024]{1,0:T(8,128)(2,1)}, bf16[256,1024]{1,0:T(8,128)(2,1)S(1)}, bf16[256,1024]{1,0:T(8,128)(2,1)S(...) custom-call(s32[1]{0:T(128)S(6)} %add.429.refs_0_, bf16[2048,1152]{1,0:T(8,128)(2,1)} %get-tuple-element.103.refs_1_.rows, ...), custom_call_target="tpu_custom_call" | custom-call | flops 6442450944 | bytes 14680064 | tf_op jit(solution)/shard_map/experts/pallas_call | solution.py:282
  401.7 13.1 %experts.13 = (bf16[2048,2048]{1,0:T(8,128)(2,1)}, bf16[2048,1024]{1,0:T(8,128)(2,1)}, bf16[256,1024]{1,0:T(8,128)(2,1)S(1)}, bf16[256,1024]{1,0:T(8,128)(2,1)S(...) custom-call(s32[1]{0:T(128)S(6)} %add.429.refs_0_, ...), custom_call_target="tpu_custom_call", output_to_operand_aliasing={{0}: (7, {}), {1}: (8, {})} | custom-call | flops 6442450944 | bytes 14680064 | tf_op jit(solution)/shard_map/experts/pallas_call | solution.py:282
  415.6 13.1 %experts.14 = (bf16[2048,2048]{1,0:T(8,128)(2,1)}, bf16[2048,1024]{1,0:T(8,128)(2,1)}, bf16[256,1024]{1,0:T(8,128)(2,1)S(1)}, bf16[256,1024]{1,0:T(8,128)(2,1)S(...) custom-call(s32[1]{0:T(128)S(6)} %add.429.refs_0_, ...), custom_call_target="tpu_custom_call", output_to_operand_aliasing={{0}: (7, {}), {1}: (8, {})} | custom-call | flops 6442450944 | bytes 14680064 | tf_op jit(solution)/shard_map/experts/pallas_call | solution.py:282
  429.5 13.3 %experts.15 = (bf16[2048,2048]{1,0:T(8,128)(2,1)}, bf16[2048,1024]{1,0:T(8,128)(2,1)}, bf16[256,1024]{1,0:T(8,128)(2,1)S(1)}, bf16[256,1024]{1,0:T(8,128)(2,1)},...) custom-call(s32[1]{0:T(128)S(6)} %add.429.refs_0_, ...), custom_call_target="tpu_custom_call", output_to_operand_aliasing={{0}: (7, {}), {1}: (8, {})} | custom-call | flops 6442450944 | bytes 14680064 | tf_op jit(solution)/shard_map/experts/pallas_call | solution.py:282
  444.3 23.0 %expert_grads.3 = (bf16[4,2,2,384,128]{4,3,2,1,0:T(8,128)(2,1)}, bf16[4,2,2,384,128]{4,3,2,1,0:T(8,128)(2,1)}, bf16[4,2,2,384,128]{4,3,2,1,0:T(8,128)(2,1)}, bf16[4,2,2,384,128]{4,3,2,1,0:T(8,128)(2,1)}) custom-call(s32[8]{0:T(128)} %copy-done.22, bf16[2048,1152]{1,0:T(8,128)(2,1)} %get-tuple-element.103.refs_1_.rows, ...), custom_call_target="tpu_custom_call" | custom-call | flops 12884901888 | bytes 20971520 | tf_op jit(solution)/shard_map/expert_grads/pallas_call | solution.py:332
  467.3 22.7 %expert_grads.2 = (bf16[4,2,2,384,128]{4,3,2,1,0:T(8,128)(2,1)}, bf16[4,2,2,384,128]{4,3,2,1,0:T(8,128)(2,1)}, bf16[4,2,2,384,128]{4,3,2,1,0:T(8,128)(2,1)}, bf16[4,2,2,384,128]{4,3,2,1,0:T(8,128)(2,1)}) custom-call(s32[8]{0:T(128)} %copy-done.22, bf16[2048,1152]{1,0:T(8,128)(2,1)} %get-tuple-element.103.refs_1_.rows, ...), custom_call_target="tpu_custom_call" | custom-call | flops 12884901888 | bytes 20971520 | tf_op jit(solution)/shard_map/expert_grads/pallas_call | solution.py:332
  506.6 9.0 %collective-permute-done.55 = bf16[256,1152]{1,0:T(8,128)(2,1)S(1)} collective-permute-done((bf16[256,1152]{1,0:T(8,128)(2,1)S(1)}, bf16[256,1152]{1,0:T(8,128)(2,1)S(1)}, u32[]{:S(2)}, u32[]{:S(2)}) %collective-permute-start.55) | collective-permute-done | bytes 589856 | tf_op jit(solution)/shard_map/ppermute | solution.py:72
  517.1 32.6 %collective-permute-done.53 = bf16[256,1152]{1,0:T(8,128)(2,1)S(1)} collective-permute-done((bf16[256,1152]{1,0:T(8,128)(2,1)S(1)}, bf16[256,1152]{1,0:T(8,128)(2,1)S(1)}, u32[]{:S(2)}, u32[]{:S(2)}) %collective-permute-start.53) | collective-permute-done | bytes 589856 | tf_op jit(solution)/shard_map/ppermute | solution.py:72
  557.6 8.9 %collective-permute-done.48 = bf16[256,1024]{1,0:T(8,128)(2,1)S(1)} collective-permute-done((bf16[256,1024]{1,0:T(8,128)(2,1)S(1)}, bf16[256,1024]{1,0:T(8,128)(2,1)S(1)}, u32[]{:S(2)}, u32[]{:S(2)}) %collective-permute-start.48) | collective-permute-done | bytes 524320 | tf_op jit(solution)/shard_map/ppermute | solution.py:72
  569.5 25.2 %collective-permute-done.46 = bf16[256,1024]{1,0:T(8,128)(2,1)S(1)} collective-permute-done((bf16[256,1024]{1,0:T(8,128)(2,1)S(1)}, bf16[256,1024]{1,0:T(8,128)(2,1)S(1)}, u32[]{:S(2)}, u32[]{:S(2)}) %collective-permute-start.46) | collective-permute-done | bytes 524320 | tf_op jit(solution)/shard_map/ppermute | solution.py:72
  598.3 34.6 %collective-permute-done.70 = f32[33,1024]{1,0:T(8,128)S(1)} collective-permute-done((f32[33,1024]{1,0:T(8,128)S(1)}, f32[33,1024]{1,0:T(8,128)S(1)}, u32[]{:S(2)}, u32[]{:S(2)}) %collective-permute-start.70) | collective-permute-done | bytes 135200 | tf_op jit(solution)/shard_map/ppermute | solution.py:72
  650.5 8.3 collective-permute-done.73
  735.1 10.7 %collective-permute-done.65 = bf16[4,128,256]{2,1,0:T(8,128)(2,1)S(1)} collective-permute-done((bf16[4,128,256]{2,1,0:T(8,128)(2,1)S(1)}, bf16[4,128,256]{2,1,0:T(8,128)(2,1)S(1)}, u32[]{:S(2)}, u32[]{:S(2)}) %collective-permute-start.65) | collective-permute-done | bytes 262176 | tf_op jit(solution)/shard_map/ppermute | solution.py:72
  767.0 16.1 %collective-permute-start.79 = (bf16[2,2,384,128]{3,2,1,0:T(8,128)(2,1)S(1)}, bf16[2,2,384,128]{3,2,1,0:T(8,128)(2,1)S(1)}, u32[]{:S(2)}, u32[]{:S(2)}) collective-permute-start(bf16[2,2,384,128]{3,2,1,0:T(8,128)(2,1)S(1)} %copy-done.105), channel_id=1, source_target_pairs={{0,16},{8,24},{16,0},{24,8},{1,17},{9,25},{17,1},{25,9},{2,18},{10... | collective-permute-start | bytes 1179656 | tf_op jit(solution)/shard_map/ppermute | solution.py:72
  783.1 22.4 %collective-permute-done.86 = bf16[2,2,384,128]{3,2,1,0:T(8,128)(2,1)} collective-permute-done((bf16[2,2,384,128]{3,2,1,0:T(8,128)(2,1)}, bf16[2,2,384,128]{3,2,1,0:T(8,128)(2,1)}, u32[]{:S(2)}, u32[]{:S(2)}) %collective-permute-start.86) | collective-permute-done | bytes 393248 | tf_op jit(solution)/shard_map/ppermute | solution.py:72
  808.9 5.7 collective-permute-start.63
  814.5 13.4 %collective-permute-done.79 = bf16[2,2,384,128]{3,2,1,0:T(8,128)(2,1)S(1)} collective-permute-done((bf16[2,2,384,128]{3,2,1,0:T(8,128)(2,1)S(1)}, bf16[2,2,384,128]{3,2,1,0:T(8,128)(2,1)S(1)}, u32[]{:S(2)}, u32[]{:S(2)}) %collective-permute-start.79) | collective-permute-done | bytes 393248 | tf_op jit(solution)/shard_map/ppermute | solution.py:72
  844.0 14.3 %expert_adam.1 = (f32[2,32,128,128]{3,2,1,0:T(8,128)}, f32[2,32,128,128]{3,2,1,0:T(8,128)}, f32[2,32,128,128]{3,2,1,0:T(8,128)}, f32[32,128,128]{2,1,0:T(8,128)}...) custom-call(s32[16]{0:T(128)S(1)} %stack.257.refs_0_, bf16[2,4,4,384,128]{4,3,2,1,0:T(8,128)(2,1)S(1)} %pad_maximum_fusion.1.refs_1_, ...), custom_call_target="tpu_custom_call" | custom-call | flops 94371840 | bytes 40894464 | tf_op jit(solution)/shard_map/expert_adam/pallas_call | solution.py:386
  (646 shorter events, 305.9 us)
Async XLA Ops:
  69.8 59.8 %collective-permute-start.7 = (bf16[2,256,1024]{2,1,0:T(8,128)(2,1)S(1)}, bf16[2,256,1024]{2,1,0:T(8,128)(2,1)S(1)}, u32[]{:S(2)}, u32[]{:S(2)}) collective-permute-start(bf16[2,256,1024]{2,1,0:T(8,128)(2,1)S(1)} %pad_maximum_fusion.6), channel_id=1, source_target_pairs={{0,1},{1,0},{2,3},{3,2},{4,5},{5,4},{6,7},{7,6},{8,9},{9,8},{10,11... | collective-permute-start | bytes 3145736 | tf_op jit(solution)/shard_map/ppermute | solution.py:72
  76.0 51.1 %collective-permute-start.15 = (bf16[2,2,384,128]{3,2,1,0:T(8,128)(2,1)S(1)}, bf16[2,2,384,128]{3,2,1,0:T(8,128)(2,1)S(1)}, u32[]{:S(2)}, u32[]{:S(2)}) collective-permute-start(bf16[2,2,384,128]{3,2,1,0:T(8,128)(2,1)S(1)} %pad_maximum_fusion.22), channel_id=1, source_target_pairs={{0,16},{8,24},{16,0},{24,8},{1,17},{9,25},{17,1},{25,9},{2,18},{10... | collective-permute-start | bytes 1179656 | tf_op jit(solution)/shard_map/ppermute | solution.py:72
  76.2 51.0 %collective-permute-start.14 = (bf16[2,2,384,128]{3,2,1,0:T(8,128)(2,1)S(1)}, bf16[2,2,384,128]{3,2,1,0:T(8,128)(2,1)S(1)}, u32[]{:S(2)}, u32[]{:S(2)}) collective-permute-start(bf16[2,2,384,128]{3,2,1,0:T(8,128)(2,1)S(1)} %pad_maximum_fusion.21), channel_id=1, source_target_pairs={{0,8},{8,0},{16,24},{24,16},{1,9},{9,1},{17,25},{25,17},{2,10},{10... | collective-permute-start | bytes 1179656 | tf_op jit(solution)/shard_map/ppermute | solution.py:72
  77.1 50.9 %collective-permute-start.35 = (bf16[2,2,384,128]{3,2,1,0:T(8,128)(2,1)S(1)}, bf16[2,2,384,128]{3,2,1,0:T(8,128)(2,1)S(1)}, u32[]{:S(2)}, u32[]{:S(2)}) collective-permute-start(bf16[2,2,384,128]{3,2,1,0:T(8,128)(2,1)S(1)} %pad_maximum_fusion.26), channel_id=1, source_target_pairs={{0,24},{8,16},{16,8},{24,0},{1,25},{9,17},{17,9},{25,1},{2,26},{10... | collective-permute-start | bytes 1179656 | tf_op jit(solution)/shard_map/ppermute | solution.py:72
  86.2 57.4 %collective-permute-start.34 = (bf16[2,2,384,128]{3,2,1,0:T(8,128)(2,1)S(1)}, bf16[2,2,384,128]{3,2,1,0:T(8,128)(2,1)S(1)}, u32[]{:S(2)}, u32[]{:S(2)}) collective-permute-start(bf16[2,2,384,128]{3,2,1,0:T(8,128)(2,1)S(1)} %pad_maximum_fusion.25), channel_id=1, source_target_pairs={{0,16},{8,24},{16,0},{24,8},{1,17},{9,25},{17,1},{25,9},{2,18},{10... | collective-permute-start | bytes 1179656 | tf_op jit(solution)/shard_map/ppermute | solution.py:72
  127.9 51.2 %collective-permute-start.19 = (bf16[4,2,384,128]{3,2,1,0:T(8,128)(2,1)S(1)}, bf16[4,2,384,128]{3,2,1,0:T(8,128)(2,1)S(1)}, u32[]{:S(2)}, u32[]{:S(2)}) collective-permute-start(bf16[4,2,384,128]{3,2,1,0:T(8,128)(2,1)S(1)} %pad_maximum_fusion.11.refs_0_), channel_id=1, source_target_pairs={{0,4},{4,0},{1,5},{5,1},{2,6},{6,2},{3,7},{7,3},{8,12},{12,8},{9,1... | collective-permute-start | bytes 2359304 | tf_op jit(solution)/shard_map/ppermute | solution.py:72
  216.9 53.3 %collective-permute-start.27 = (bf16[256,1152]{1,0:T(8,128)(2,1)S(1)}, bf16[256,1152]{1,0:T(8,128)(2,1)}, u32[]{:S(2)}, u32[]{:S(2)}) collective-permute-start(bf16[256,1152]{1,0:T(8,128)(2,1)S(1)} %concatenate.121.refs_1_), channel_id=1, source_target_pairs={{0,8},{8,0},{16,24},{24,16},{1,9},{9,1},{17,25},{25,17},{2,10},{10... | collective-permute-start | bytes 1769480 | tf_op jit(solution)/shard_map/ppermute | solution.py:72
  267.0 52.1 %collective-permute-start.25 = (bf16[256,1024]{1,0:T(8,128)(2,1)}, bf16[256,1024]{1,0:T(8,128)(2,1)S(1)}, u32[]{:S(2)}, u32[]{:S(2)}) collective-permute-start(bf16[256,1024]{1,0:T(8,128)(2,1)} %convert_element_type.348.refs_3_), channel_id=1, source_target_pairs={{0,16},{8,24},{16,0},{24,8},{1,17},{9,25},{17,1},{25,9},{2,18},{10... | collective-permute-start | bytes 1572872 | tf_op jit(solution)/shard_map/ppermute | solution.py:72
  268.5 50.6 %collective-permute-start.30 = (bf16[256,1024]{1,0:T(8,128)(2,1)}, bf16[256,1024]{1,0:T(8,128)(2,1)S(1)}, u32[]{:S(2)}, u32[]{:S(2)}) collective-permute-start(bf16[256,1024]{1,0:T(8,128)(2,1)} %collective-permute-done.29.refs_3_), channel_id=1, source_target_pairs={{0,1},{1,0},{2,3},{3,2},{4,5},{5,4},{6,7},{7,6},{8,9},{9,8},{10,11... | collective-permute-start | bytes 1572872 | tf_op jit(solution)/shard_map/ppermute | solution.py:72
  268.7 50.9 %collective-permute-start.9 = (bf16[256,1152]{1,0:T(8,128)(2,1)S(1)}, bf16[256,1152]{1,0:T(8,128)(2,1)S(1)}, u32[]{:S(2)}, u32[]{:S(2)}) collective-permute-start(bf16[256,1152]{1,0:T(8,128)(2,1)S(1)} %concatenate.121.refs_1_), channel_id=1, source_target_pairs={{0,24},{8,16},{16,8},{24,0},{1,25},{9,17},{17,9},{25,1},{2,26},{10... | collective-permute-start | bytes 1769480 | tf_op jit(solution)/shard_map/ppermute | solution.py:72
  270.1 74.1 %collective-permute-start.23 = (bf16[256,1152]{1,0:T(8,128)(2,1)S(1)}, bf16[256,1152]{1,0:T(8,128)(2,1)S(1)}, u32[]{:S(2)}, u32[]{:S(2)}) collective-permute-start(bf16[256,1152]{1,0:T(8,128)(2,1)S(1)} %concatenate.121.refs_1_), channel_id=1, source_target_pairs={{0,16},{8,24},{16,0},{24,8},{1,17},{9,25},{17,1},{25,9},{2,18},{10... | collective-permute-start | bytes 1769480 | tf_op jit(solution)/shard_map/ppermute | solution.py:72
  271.6 72.6 %collective-permute-start.28 = (bf16[256,1152]{1,0:T(8,128)(2,1)}, bf16[256,1152]{1,0:T(8,128)(2,1)S(1)}, u32[]{:S(2)}, u32[]{:S(2)}) collective-permute-start(bf16[256,1152]{1,0:T(8,128)(2,1)} %collective-permute-done.27.refs_1_), channel_id=1, source_target_pairs={{0,1},{1,0},{2,3},{3,2},{4,5},{5,4},{6,7},{7,6},{8,9},{9,8},{10,11... | collective-permute-start | bytes 1769480 | tf_op jit(solution)/shard_map/ppermute | solution.py:72
  319.0 54.0 %collective-permute-start.12 = (bf16[256,1024]{1,0:T(8,128)(2,1)}, bf16[256,1024]{1,0:T(8,128)(2,1)S(1)}, u32[]{:S(2)}, u32[]{:S(2)}) collective-permute-start(bf16[256,1024]{1,0:T(8,128)(2,1)} %collective-permute-done.11.refs_3_), channel_id=1, source_target_pairs={{0,1},{1,0},{2,3},{3,2},{4,5},{5,4},{6,7},{7,6},{8,9},{9,8},{10,11... | collective-permute-start | bytes 1572872 | tf_op jit(solution)/shard_map/ppermute | solution.py:72
  319.5 53.5 %collective-permute-start.10 = (bf16[256,1152]{1,0:T(8,128)(2,1)S(1)}, bf16[256,1152]{1,0:T(8,128)(2,1)S(1)}, u32[]{:S(2)}, u32[]{:S(2)}) collective-permute-start(bf16[256,1152]{1,0:T(8,128)(2,1)S(1)} %collective-permute-done.9.refs_1_), channel_id=1, source_target_pairs={{0,1},{1,0},{2,3},{3,2},{4,5},{5,4},{6,7},{7,6},{8,9},{9,8},{10,11... | collective-permute-start | bytes 1769480 | tf_op jit(solution)/shard_map/ppermute | solution.py:72
  442.7 51.0 %collective-permute-start.54 = (bf16[256,1152]{1,0:T(8,128)(2,1)}, bf16[256,1152]{1,0:T(8,128)(2,1)}, u32[]{:S(2)}, u32[]{:S(2)}) collective-permute-start(bf16[256,1152]{1,0:T(8,128)(2,1)} %get-tuple-element.136), channel_id=1, source_target_pairs={{0,1},{1,0},{2,3},{3,2},{4,5},{5,4},{6,7},{7,6},{8,9},{9,8},{10,11... | collective-permute-start | bytes 1769480 | tf_op jit(solution)/shard_map/ppermute | solution.py:72
  443.3 52.4 %collective-permute-start.52 = (bf16[256,1152]{1,0:T(8,128)(2,1)}, bf16[256,1152]{1,0:T(8,128)(2,1)}, u32[]{:S(2)}, u32[]{:S(2)}) collective-permute-start(bf16[256,1152]{1,0:T(8,128)(2,1)} %get-tuple-element.134), channel_id=1, source_target_pairs={{0,1},{1,0},{2,3},{3,2},{4,5},{5,4},{6,7},{7,6},{8,9},{9,8},{10,11... | collective-permute-start | bytes 1769480 | tf_op jit(solution)/shard_map/ppermute | solution.py:72
  443.4 54.0 %collective-permute-start.50 = (bf16[256,1152]{1,0:T(8,128)(2,1)S(1)}, bf16[256,1152]{1,0:T(8,128)(2,1)}, u32[]{:S(2)}, u32[]{:S(2)}) collective-permute-start(bf16[256,1152]{1,0:T(8,128)(2,1)S(1)} %get-tuple-element.132), channel_id=1, source_target_pairs={{0,1},{1,0},{2,3},{3,2},{4,5},{5,4},{6,7},{7,6},{8,9},{9,8},{10,11... | collective-permute-start | bytes 1769480 | tf_op jit(solution)/shard_map/ppermute | solution.py:72
  443.8 61.2 %collective-permute-start.49 = (bf16[256,1152]{1,0:T(8,128)(2,1)S(1)}, bf16[256,1152]{1,0:T(8,128)(2,1)}, u32[]{:S(2)}, u32[]{:S(2)}) collective-permute-start(bf16[256,1152]{1,0:T(8,128)(2,1)S(1)} %get-tuple-element.130), channel_id=1, source_target_pairs={{0,1},{1,0},{2,3},{3,2},{4,5},{5,4},{6,7},{7,6},{8,9},{9,8},{10,11... | collective-permute-start | bytes 1769480 | tf_op jit(solution)/shard_map/ppermute | solution.py:72
  443.9 57.2 %collective-permute-start.47 = (bf16[256,1024]{1,0:T(8,128)(2,1)}, bf16[256,1024]{1,0:T(8,128)(2,1)}, u32[]{:S(2)}, u32[]{:S(2)}) collective-permute-start(bf16[256,1024]{1,0:T(8,128)(2,1)} %get-tuple-element.128), channel_id=1, source_target_pairs={{0,1},{1,0},{2,3},{3,2},{4,5},{5,4},{6,7},{7,6},{8,9},{9,8},{10,11... | collective-permute-start | bytes 1572872 | tf_op jit(solution)/shard_map/ppermute | solution.py:72
  501.2 49.9 %collective-permute-start.51 = (bf16[256,1152]{1,0:T(8,128)(2,1)S(1)}, bf16[256,1152]{1,0:T(8,128)(2,1)S(1)}, u32[]{:S(2)}, u32[]{:S(2)}) collective-permute-start(bf16[256,1152]{1,0:T(8,128)(2,1)S(1)} %add_convert_fusion.6), channel_id=1, source_target_pairs={{0,8},{8,0},{16,24},{24,16},{1,9},{9,1},{17,25},{25,17},{2,10},{10... | collective-permute-start | bytes 1769480 | tf_op jit(solution)/shard_map/ppermute | solution.py:72
  504.7 49.9 %collective-permute-start.42 = (bf16[256,1024]{1,0:T(8,128)(2,1)S(1)}, bf16[256,1024]{1,0:T(8,128)(2,1)S(1)}, u32[]{:S(2)}, u32[]{:S(2)}) collective-permute-start(bf16[256,1024]{1,0:T(8,128)(2,1)S(1)} %copy-done.24), channel_id=1, source_target_pairs={{0,1},{1,0},{2,3},{3,2},{4,5},{5,4},{6,7},{7,6},{8,9},{9,8},{10,11... | collective-permute-start | bytes 1572872 | tf_op jit(solution)/shard_map/ppermute | solution.py:72
  505.0 129.4 %collective-permute-start.81 = (bf16[4,2,2,384,128]{4,3,2,0,1:T(8,128)(2,1)S(1)}, bf16[4,2,2,384,128]{4,3,2,0,1:T(8,128)(2,1)S(1)}, u32[]{:S(2)}, u32[]{:S(2)}) collective-permute-start(bf16[4,2,2,384,128]{4,3,2,0,1:T(8,128)(2,1)S(1)} %copy.185), channel_id=1, source_target_pairs={{0,4},{4,0},{1,5},{5,1},{2,6},{6,2},{3,7},{7,3},{8,12},{12,8},{9,1... | collective-permute-start | bytes 4718600 | tf_op jit(solution)/shard_map/ppermute | solution.py:72
  515.6 120.3 %collective-permute-start.83 = (bf16[4,2,2,384,128]{4,3,2,0,1:T(8,128)(2,1)S(1)}, bf16[4,2,2,384,128]{4,3,2,0,1:T(8,128)(2,1)S(1)}, u32[]{:S(2)}, u32[]{:S(2)}) collective-permute-start(bf16[4,2,2,384,128]{4,3,2,0,1:T(8,128)(2,1)S(1)} %copy.187), channel_id=1, source_target_pairs={{0,2},{2,0},{1,3},{3,1},{4,6},{6,4},{5,7},{7,5},{8,10},{10,8},{9,1... | collective-permute-start | bytes 4718600 | tf_op jit(solution)/shard_map/ppermute | solution.py:72
  567.9 70.0 %collective-permute-start.74 = (bf16[4,2,2,384,128]{4,3,2,0,1:T(8,128)(2,1)S(1)}, bf16[4,2,2,384,128]{4,3,2,0,1:T(8,128)(2,1)S(1)}, u32[]{:S(2)}, u32[]{:S(2)}) collective-permute-start(bf16[4,2,2,384,128]{4,3,2,0,1:T(8,128)(2,1)S(1)} %copy.178), channel_id=1, source_target_pairs={{0,4},{4,0},{1,5},{5,1},{2,6},{6,2},{3,7},{7,3},{8,12},{12,8},{9,1... | collective-permute-start | bytes 4718600 | tf_op jit(solution)/shard_map/ppermute | solution.py:72
  638.0 87.7 %collective-permute-start.82 = (bf16[4,2,384,128]{3,2,1,0:T(8,128)(2,1)}, bf16[4,2,384,128]{3,2,1,0:T(8,128)(2,1)}, u32[]{:S(2)}, u32[]{:S(2)}) collective-permute-start(bf16[4,2,384,128]{3,2,1,0:T(8,128)(2,1)} %slice_bitcast_fusion.9), channel_id=1, source_target_pairs={{0,2},{2,0},{1,3},{3,1},{4,6},{6,4},{5,7},{7,5},{8,10},{10,8},{9,1... | collective-permute-start | bytes 2359304 | tf_op jit(solution)/shard_map/ppermute | solution.py:72
  640.4 87.4 %collective-permute-start.84 = (bf16[4,2,384,128]{3,2,1,0:T(8,128)(2,1)}, bf16[4,2,384,128]{3,2,1,0:T(8,128)(2,1)}, u32[]{:S(2)}, u32[]{:S(2)}) collective-permute-start(bf16[4,2,384,128]{3,2,1,0:T(8,128)(2,1)} %slice_bitcast_fusion.7), channel_id=1, source_target_pairs={{0,4},{4,0},{1,5},{5,1},{2,6},{6,2},{3,7},{7,3},{8,12},{12,8},{9,1... | collective-permute-start | bytes 2359304 | tf_op jit(solution)/shard_map/ppermute | solution.py:72
  658.8 72.9 %collective-permute-start.75 = (bf16[4,2,384,128]{3,2,1,0:T(8,128)(2,1)}, bf16[4,2,384,128]{3,2,1,0:T(8,128)(2,1)}, u32[]{:S(2)}, u32[]{:S(2)}) collective-permute-start(bf16[4,2,384,128]{3,2,1,0:T(8,128)(2,1)} %slice_bitcast_fusion.14), channel_id=1, source_target_pairs={{0,2},{2,0},{1,3},{3,1},{4,6},{6,4},{5,7},{7,5},{8,10},{10,8},{9,1... | collective-permute-start | bytes 2359304 | tf_op jit(solution)/shard_map/ppermute | solution.py:72
  661.7 72.0 %collective-permute-start.77 = (bf16[4,2,384,128]{3,2,1,0:T(8,128)(2,1)}, bf16[4,2,384,128]{3,2,1,0:T(8,128)(2,1)}, u32[]{:S(2)}, u32[]{:S(2)}) collective-permute-start(bf16[4,2,384,128]{3,2,1,0:T(8,128)(2,1)} %slice_bitcast_fusion.12), channel_id=1, source_target_pairs={{0,4},{4,0},{1,5},{5,1},{2,6},{6,2},{3,7},{7,3},{8,12},{12,8},{9,1... | collective-permute-start | bytes 2359304 | tf_op jit(solution)/shard_map/ppermute | solution.py:72
  724.9 111.2 %collective-permute-start.59 = (bf16[2,256,1024]{2,1,0:T(8,128)(2,1)}, bf16[2,256,1024]{2,1,0:T(8,128)(2,1)}, u32[]{:S(2)}, u32[]{:S(2)}) collective-permute-start(bf16[2,256,1024]{2,1,0:T(8,128)(2,1)} %pad_maximum_fusion.9), channel_id=1, source_target_pairs={{0,1},{1,0},{2,3},{3,2},{4,5},{5,4},{6,7},{7,6},{8,9},{9,8},{10,11... | collective-permute-start | bytes 3145736 | tf_op jit(solution)/shard_map/ppermute | solution.py:72
  754.5 51.0 %collective-permute-start.86 = (bf16[2,2,384,128]{3,2,1,0:T(8,128)(2,1)}, bf16[2,2,384,128]{3,2,1,0:T(8,128)(2,1)}, u32[]{:S(2)}, u32[]{:S(2)}) collective-permute-start(bf16[2,2,384,128]{3,2,1,0:T(8,128)(2,1)} %get-tuple-element.266), channel_id=1, source_target_pairs={{0,16},{8,24},{16,0},{24,8},{1,17},{9,25},{17,1},{25,9},{2,18},{10... | collective-permute-start | bytes 1179656 | tf_op jit(solution)/shard_map/ppermute | solution.py:72
  754.5 51.0 %collective-permute-start.85 = (bf16[2,2,384,128]{3,2,1,0:T(8,128)(2,1)}, bf16[2,2,384,128]{3,2,1,0:T(8,128)(2,1)}, u32[]{:S(2)}, u32[]{:S(2)}) collective-permute-start(bf16[2,2,384,128]{3,2,1,0:T(8,128)(2,1)} %get-tuple-element.264), channel_id=1, source_target_pairs={{0,8},{8,0},{16,24},{24,16},{1,9},{9,1},{17,25},{25,17},{2,10},{10... | collective-permute-start | bytes 1179656 | tf_op jit(solution)/shard_map/ppermute | solution.py:72
  767.0 60.9 %collective-permute-start.79 = (bf16[2,2,384,128]{3,2,1,0:T(8,128)(2,1)S(1)}, bf16[2,2,384,128]{3,2,1,0:T(8,128)(2,1)S(1)}, u32[]{:S(2)}, u32[]{:S(2)}) collective-permute-start(bf16[2,2,384,128]{3,2,1,0:T(8,128)(2,1)S(1)} %copy-done.105), channel_id=1, source_target_pairs={{0,16},{8,24},{16,0},{24,8},{1,17},{9,25},{17,1},{25,9},{2,18},{10... | collective-permute-start | bytes 1179656 | tf_op jit(solution)/shard_map/ppermute | solution.py:72
  (205 other events, 2828.1 us)
